TPU v7x, 512 devices: a whole 4x8x8 slice. The times are simulated.
512 devices in a mesh: chrom: 256 (over z_hi, x, y, core), chan: 2 (over z_lo).
Axes of the slice: x: 4, y: 8, z: 8 (z_hi: 4, z_lo: 2; z = z_hi * 2 + z_lo), core: 2. Of those that a mesh axis runs over, the one named last changes fastest.
Arguments:
- left_embed: bfloat16 [4096, 256], P('chrom', 'chan'), may hold values from -6 to 6
- right_embed: bfloat16 [4096, 256], P('chrom', 'chan'), may hold values from -6 to 6
- conv_weight: bfloat16 [3, 3, 3, 256, 256], P(None, None, None, None, 'chan'), may hold values from -0.125 to 0.125
- readout: float32 [256], P('chan'), may hold values from -0.375 to 0.375
- cotangent: float32 [4096, 64], P('chrom'), may hold values from -6 to 6
Outputs:
- contact: float32 [4096, 64], P('chrom')
- left_grad: float32 [4096, 256], P('chrom', 'chan')
- right_grad: float32 [4096, 256], P('chrom', 'chan')
All inputs are finite; a program needn't handle non-finite values.
Results may differ from a plain program's by a relative error of at most 0.013.
Values may be sent and summed in bfloat16 or wider, within the bound.
No kernel may reach another device: no remote copies, remote signals or barrier semaphores. Data moves between devices by JAX's collectives and lax.ppermute only.
A program may use at most 64 MiB of HBM per device.

v0:
```python
import jax
import jax.numpy as jnp
from jax import lax
from jax.sharding import PartitionSpec as P


def passed_along(value, axis, steps):
    count = lax.axis_size(axis)
    initial, last = (max(0, -steps), min(count, count - steps))
    return lax.ppermute(value, axis, [(source, source + steps) for source in range(initial, last)])


def padded_2(array, sides, width):
    for axis, dim in sides:
        devices, length = (lax.axis_size(axis), array.shape[dim])
        up = [(i, (i + 1) % devices) for i in range(devices - 1)]
        down = [(j, i) for i, j in up]
        last = lax.slice_in_dim(array, length - width, length, axis=dim)
        initial = lax.slice_in_dim(array, 0, width, axis=dim)
        before = lax.ppermute(last, axis, up)
        after = lax.ppermute(initial, axis, down)
        array = jnp.concatenate([before, array, after], axis=dim)
    return array


def silu_grad(z):
    s = jax.nn.sigmoid(z)
    return s * (1.0 + z * (1.0 - s))


def local(left_embed, right_embed, conv_weight, readout, cotangent):
    rows, share = left_embed.shape
    band = cotangent.shape[1]
    slabs = band // rows
    layers = conv_weight.shape[0]
    channels = conv_weight.shape[3]

    def pass_along(carry, unused):
        moved = passed_along(carry, "chrom", -1)
        return (moved, moved)

    unused_last, later = lax.scan(pass_along, right_embed, None, length=slabs)
    right_band = jnp.concatenate([right_embed[None], later], axis=0).reshape(-1, share)
    left_wide = left_embed.astype(jnp.float32)
    pair = jnp.stack(
        [
            left_wide[row][None, :] + right_band[row : row + band].astype(jnp.float32)
            for row in range(rows)
        ]
    ).astype(jnp.bfloat16)
    states = []
    for layer in range(layers):
        r = 2**layer
        rimmed = padded_2(pair, (("chrom", 0),), r)
        full = lax.all_gather(rimmed, "chan", axis=2, tiled=True)
        padded = jnp.pad(full, ((0, 0), (r, r), (0, 0)))
        pre = jnp.zeros((rows, band, share), jnp.float32)
        for a in range(3):
            for b in range(3):
                piece = padded[a * r : a * r + rows, b * r : b * r + band, :]
                pre = pre + jnp.dot(
                    piece, conv_weight[layer, a, b], preferred_element_type=jnp.float32
                )
        states.append(pre)
        pair = (pair.astype(jnp.float32) + jax.nn.silu(pre)).astype(jnp.bfloat16)
    contact = lax.psum(jnp.sum(pair.astype(jnp.float32) * readout[None, None, :], axis=-1), "chan")
    grad = cotangent[:, :, None] * readout[None, None, :]
    for layer in reversed(range(layers)):
        r = 2**layer
        dpre = (grad * silu_grad(states[layer])).astype(jnp.bfloat16)
        rimmed = padded_2(dpre, (("chrom", 0),), r)
        padded = jnp.pad(rimmed, ((0, 0), (r, r), (0, 0)))
        part = jnp.zeros((rows, band, channels), jnp.float32)
        for a in range(3):
            for b in range(3):
                piece = padded[
                    (2 - a) * r : (2 - a) * r + rows, (2 - b) * r : (2 - b) * r + band, :
                ]
                part = part + jnp.einsum(
                    "xyo,io->xyi",
                    piece,
                    conv_weight[layer, a, b],
                    preferred_element_type=jnp.float32,
                )
        grad = grad + lax.psum_scatter(
            part.astype(jnp.bfloat16), "chan", scatter_dimension=2, tiled=True
        ).astype(jnp.float32)
    left_grad = jnp.sum(grad, axis=1)
    spread = jnp.zeros((band + rows, share), jnp.float32)
    for row in range(rows):
        spread = spread.at[row : row + band].add(grad[row])
    blocks = spread.reshape(slabs + 1, rows, share)

    def carry_terms(carry, block):
        moved = passed_along(carry + block, "chrom", 1)
        return (moved, None)

    arrived, unused_out = lax.scan(
        carry_terms, jnp.zeros((rows, share), jnp.float32), blocks[1:][::-1]
    )
    right_grad = blocks[0] + arrived
    return (contact, left_grad, right_grad)


def solution(mesh):
    return jax.shard_map(
        local,
        mesh=mesh,
        in_specs=(
            P("chrom", "chan"),
            P("chrom", "chan"),
            P(None, None, None, None, "chan"),
            P("chan"),
            P("chrom", None),
        ),
        out_specs=(P("chrom", None), P("chrom", "chan"), P("chrom", "chan")),
        check_vma=False,
    )
```

profile of v0, /device:TPU:256, one launch (start us, length us, event | category | flops | bytes accessed | tf_op | source)
XLA Modules:
  0.0 313.7 jit_solution(1613256231251140775)
XLA Ops:
  8.0 40.3 %while.38 = (s32[]{:T(128)}, bf16[16,128]{1,0:T(8,128)(2,1)S(1)}, bf16[4,16,128]{2,1,0:T(8,128)(2,1)S(1)}, s32[]{:T(128)}) while((s32[]{:T(128)}, bf16[16,128]{1,0:T(8,128)(2,1)S(1)}, bf16[4,16,128]{2,1,0:T(8,128)(2,1)S(1)}, s32[]{:T(128)}) %tuple.125), condition=%wide.region_1.2_spmd, body=%wide.region_0.1_spmd.sunk | while | flops 2 | bytes 32873 | solution.py:42
  8.0 5.2 %collective-permute-start = (bf16[16,128]{1,0:T(8,128)(2,1)S(1)}, bf16[16,128]{1,0:T(8,128)(2,1)S(1)}, u32[]{:S(2)}, u32[]{:S(2)}) collective-permute-start(bf16[16,128]{1,0:T(8,128)(2,1)S(1)} %get-tuple-element.324), channel_id=1, source_target_pairs={{2,0},{4,2},{6,4},{8,6},{10,8},{12,10},{14,12},{16,14},{18,16},{20... | collective-permute-start | bytes 12296 | tf_op jit(solution)/shard_map/while/body/eval_jaxpr/ppermute | solution.py:10
  14.5 9.9 %collective-permute-start = (bf16[16,128]{1,0:T(8,128)(2,1)S(1)}, bf16[16,128]{1,0:T(8,128)(2,1)S(1)}, u32[]{:S(2)}, u32[]{:S(2)}) collective-permute-start(bf16[16,128]{1,0:T(8,128)(2,1)S(1)} %get-tuple-element.324), channel_id=1, source_target_pairs={{2,0},{4,2},{6,4},{8,6},{10,8},{12,10},{14,12},{16,14},{18,16},{20... | collective-permute-start | bytes 12296 | tf_op jit(solution)/shard_map/while/body/eval_jaxpr/ppermute | solution.py:10
  25.8 9.9 %collective-permute-start = (bf16[16,128]{1,0:T(8,128)(2,1)S(1)}, bf16[16,128]{1,0:T(8,128)(2,1)S(1)}, u32[]{:S(2)}, u32[]{:S(2)}) collective-permute-start(bf16[16,128]{1,0:T(8,128)(2,1)S(1)} %get-tuple-element.324), channel_id=1, source_target_pairs={{2,0},{4,2},{6,4},{8,6},{10,8},{12,10},{14,12},{16,14},{18,16},{20... | collective-permute-start | bytes 12296 | tf_op jit(solution)/shard_map/while/body/eval_jaxpr/ppermute | solution.py:10
  37.0 9.9 %collective-permute-start = (bf16[16,128]{1,0:T(8,128)(2,1)S(1)}, bf16[16,128]{1,0:T(8,128)(2,1)S(1)}, u32[]{:S(2)}, u32[]{:S(2)}) collective-permute-start(bf16[16,128]{1,0:T(8,128)(2,1)S(1)} %get-tuple-element.324), channel_id=1, source_target_pairs={{2,0},{4,2},{6,4},{8,6},{10,8},{12,10},{14,12},{16,14},{18,16},{20... | collective-permute-start | bytes 12296 | tf_op jit(solution)/shard_map/while/body/eval_jaxpr/ppermute | solution.py:10
  50.7 1.9 collective-permute-start.2
  52.7 10.0 %collective-permute-start.3 = (bf16[1,64,128]{2,1,0:T(8,128)(2,1)S(1)}, bf16[1,64,128]{2,1,0:T(8,128)(2,1)S(1)}, u32[]{:S(2)}, u32[]{:S(2)}) collective-permute-start(bf16[1,64,128]{2,1,0:T(8,128)(2,1)S(1)} %get-tuple-element.248), channel_id=1, source_target_pairs={{2,0},{4,2},{6,4},{8,6},{10,8},{12,10},{14,12},{16,14},{18,16},{20... | collective-permute-start | bytes 49160 | tf_op jit(solution)/shard_map/ppermute | solution.py:21
  64.1 7.8 %all_gather.9 = bf16[18,64,256]{2,1,0:T(8,128)(2,1)S(1)} all-gather(bf16[18,64,128]{2,1,0:T(8,128)(2,1)S(1)} %constant_dynamic-update-slice_fusion.16), channel_id=1, replica_groups=mesh['chrom'=256,'chan'=2] {'chan'}, dimensions={2}, use_global_device_ids=true | all-gather | bytes 884736 | tf_op jit(solution)/shard_map/all_gather | solution.py:55
  77.5 10.0 %collective-permute-start.5 = (bf16[2,64,128]{2,1,0:T(8,128)(2,1)S(1)}, bf16[2,64,128]{2,1,0:T(8,128)(2,1)S(1)}, u32[]{:S(2)}, u32[]{:S(2)}) collective-permute-start(bf16[2,64,128]{2,1,0:T(8,128)(2,1)S(1)} %get-tuple-element.260), channel_id=1, source_target_pairs={{2,0},{4,2},{6,4},{8,6},{10,8},{12,10},{14,12},{16,14},{18,16},{20... | collective-permute-start | bytes 98312 | tf_op jit(solution)/shard_map/ppermute | solution.py:21
  89.1 7.8 %all_gather.10 = bf16[20,64,256]{2,1,0:T(8,128)(2,1)S(1)} all-gather(bf16[20,64,128]{2,1,0:T(8,128)(2,1)S(1)} %pad_maximum_fusion.1), channel_id=1, replica_groups=mesh['chrom'=256,'chan'=2] {'chan'}, dimensions={2}, use_global_device_ids=true | all-gather | bytes 983040 | tf_op jit(solution)/shard_map/all_gather | solution.py:55
  100.6 1.9 collective-permute-start.6
  102.5 10.0 %collective-permute-start.7 = (bf16[4,64,128]{2,1,0:T(8,128)(2,1)S(1)}, bf16[4,64,128]{2,1,0:T(8,128)(2,1)S(1)}, u32[]{:S(2)}, u32[]{:S(2)}) collective-permute-start(bf16[4,64,128]{2,1,0:T(8,128)(2,1)S(1)} %get-tuple-element.258), channel_id=1, source_target_pairs={{2,0},{4,2},{6,4},{8,6},{10,8},{12,10},{14,12},{16,14},{18,16},{20... | collective-permute-start | bytes 196616 | tf_op jit(solution)/shard_map/ppermute | solution.py:21
  114.4 8.5 %all_gather.11 = bf16[24,64,256]{2,1,0:T(8,128)(2,1)S(1)} all-gather(bf16[24,64,128]{2,1,0:T(8,128)(2,1)S(1)} %pad_maximum_fusion), channel_id=1, replica_groups=mesh['chrom'=256,'chan'=2] {'chan'}, dimensions={2}, use_global_device_ids=true | all-gather | bytes 1179648 | tf_op jit(solution)/shard_map/all_gather | solution.py:55
  126.4 9.2 %collective-permute-start.9 = (bf16[4,64,128]{2,1,0:T(8,128)(2,1)S(1)}, bf16[4,64,128]{2,1,0:T(8,128)(2,1)S(1)}, u32[]{:S(2)}, u32[]{:S(2)}) collective-permute-start(bf16[4,64,128]{2,1,0:T(8,128)(2,1)S(1)} %get-tuple-element.256), channel_id=1, source_target_pairs={{2,0},{4,2},{6,4},{8,6},{10,8},{12,10},{14,12},{16,14},{18,16},{20... | collective-permute-start | bytes 196616 | tf_op jit(solution)/shard_map/ppermute | solution.py:21
  137.5 10.4 %collective-permute-done.8 = bf16[4,64,128]{2,1,0:T(8,128)(2,1)S(1)} collective-permute-done((bf16[4,64,128]{2,1,0:T(8,128)(2,1)S(1)}, bf16[4,64,128]{2,1,0:T(8,128)(2,1)S(1)}, u32[]{:S(2)}, u32[]{:S(2)}) %collective-permute-start.8) | collective-permute-done | bytes 65568 | tf_op jit(solution)/shard_map/ppermute | solution.py:20
  153.5 15.9 %reduce-scatter.10.cloned.1.call-done = bf16[128,1024]{1,0:T(8,128)(2,1)} async-done(((bf16[256,1024]{1,0:T(8,128)(2,1)}), bf16[128,1024]{1,0:T(8,128)(2,1)}) %reduce-scatter.10.cloned.1.call-update) | async-done | bytes 262160
  171.4 6.8 %collective-permute-start.11 = (bf16[2,64,128]{2,1,0:T(8,128)(2,1)S(1)}, bf16[2,64,128]{2,1,0:T(8,128)(2,1)S(1)}, u32[]{:S(2)}, u32[]{:S(2)}) collective-permute-start(bf16[2,64,128]{2,1,0:T(8,128)(2,1)S(1)} %get-tuple-element.254), channel_id=1, source_target_pairs={{2,0},{4,2},{6,4},{8,6},{10,8},{12,10},{14,12},{16,14},{18,16},{20... | collective-permute-start | bytes 98312 | tf_op jit(solution)/shard_map/ppermute | solution.py:21
  178.3 1.9 collective-permute-start.10
  180.2 9.6 %collective-permute-done.10 = bf16[2,64,128]{2,1,0:T(8,128)(2,1)S(1)} collective-permute-done((bf16[2,64,128]{2,1,0:T(8,128)(2,1)S(1)}, bf16[2,64,128]{2,1,0:T(8,128)(2,1)S(1)}, u32[]{:S(2)}, u32[]{:S(2)}) %collective-permute-start.10) | collective-permute-done | bytes 32800 | tf_op jit(solution)/shard_map/ppermute | solution.py:20
  193.5 2.0 copy.10
  197.1 15.8 %reduce-scatter.12.cloned.1.call-done = bf16[128,1024]{1,0:T(8,128)(2,1)} async-done(((bf16[256,1024]{1,0:T(8,128)(2,1)}), bf16[128,1024]{1,0:T(8,128)(2,1)}) %reduce-scatter.12.cloned.1.call-update) | async-done | bytes 262160
  215.1 6.8 %collective-permute-start.13 = (bf16[1,64,128]{2,1,0:T(8,128)(2,1)S(1)}, bf16[1,64,128]{2,1,0:T(8,128)(2,1)S(1)}, u32[]{:S(2)}, u32[]{:S(2)}) collective-permute-start(bf16[1,64,128]{2,1,0:T(8,128)(2,1)S(1)} %get-tuple-element.252), channel_id=1, source_target_pairs={{2,0},{4,2},{6,4},{8,6},{10,8},{12,10},{14,12},{16,14},{18,16},{20... | collective-permute-start | bytes 49160 | tf_op jit(solution)/shard_map/ppermute | solution.py:21
  221.9 1.9 collective-permute-start.12
  223.9 9.4 %collective-permute-done.12 = bf16[1,64,128]{2,1,0:T(8,128)(2,1)S(1)} collective-permute-done((bf16[1,64,128]{2,1,0:T(8,128)(2,1)S(1)}, bf16[1,64,128]{2,1,0:T(8,128)(2,1)S(1)}, u32[]{:S(2)}, u32[]{:S(2)}) %collective-permute-start.12) | collective-permute-done | bytes 16416 | tf_op jit(solution)/shard_map/ppermute | solution.py:20
  238.7 5.6 %psum.7 = f32[16,64]{1,0:T(8,128)} all-reduce(f32[16,64]{1,0:T(8,128)S(1)} %get-tuple-element.250), channel_id=1, replica_groups=mesh['chrom'=256,'chan'=2] {'chan'}, use_global_device_ids=true, to_apply=%region_3.4 | all-reduce | flops 1024 | bytes 8192 | tf_op jit(solution)/shard_map/psum | solution.py:66
  244.3 10.3 %reduce-scatter.14.cloned.1.call-done = bf16[128,1024]{1,0:T(8,128)(2,1)} async-done(((bf16[256,1024]{1,0:T(8,128)(2,1)}), bf16[128,1024]{1,0:T(8,128)(2,1)}) %reduce-scatter.14.cloned.1.call-update) | async-done | bytes 262160
  261.4 45.2 %while.39 = (s32[]{:T(128)}, f32[16,128]{1,0:T(8,128)S(1)}, f32[4,16,128]{2,1,0:T(8,128)S(1)}, s32[]{:T(128)}) while((s32[]{:T(128)}, f32[16,128]{1,0:T(8,128)S(1)}, f32[4,16,128]{2,1,0:T(8,128)S(1)}, s32[]{:T(128)}) %tuple.128), condition=%wide.region_9.10_spmd, body=%wide.region_8.9_spmd.sunk | while | flops 2050 | bytes 57441 | solution.py:98
  261.4 1.9 collective-permute-start.1
  263.3 9.4 %collective-permute-done.1 = f32[16,128]{1,0:T(8,128)S(1)} collective-permute-done((f32[16,128]{1,0:T(8,128)S(1)}, f32[16,128]{1,0:T(8,128)S(1)}, u32[]{:S(2)}, u32[]{:S(2)}) %collective-permute-start.1) | collective-permute-done | bytes 8224 | tf_op jit(solution)/shard_map/while/body/eval_jaxpr/ppermute | solution.py:10
  274.6 9.4 %collective-permute-done.1 = f32[16,128]{1,0:T(8,128)S(1)} collective-permute-done((f32[16,128]{1,0:T(8,128)S(1)}, f32[16,128]{1,0:T(8,128)S(1)}, u32[]{:S(2)}, u32[]{:S(2)}) %collective-permute-start.1) | collective-permute-done | bytes 8224 | tf_op jit(solution)/shard_map/while/body/eval_jaxpr/ppermute | solution.py:10
  285.9 9.4 %collective-permute-done.1 = f32[16,128]{1,0:T(8,128)S(1)} collective-permute-done((f32[16,128]{1,0:T(8,128)S(1)}, f32[16,128]{1,0:T(8,128)S(1)}, u32[]{:S(2)}, u32[]{:S(2)}) %collective-permute-start.1) | collective-permute-done | bytes 8224 | tf_op jit(solution)/shard_map/while/body/eval_jaxpr/ppermute | solution.py:10
  297.2 9.4 %collective-permute-done.1 = f32[16,128]{1,0:T(8,128)S(1)} collective-permute-done((f32[16,128]{1,0:T(8,128)S(1)}, f32[16,128]{1,0:T(8,128)S(1)}, u32[]{:S(2)}, u32[]{:S(2)}) %collective-permute-start.1) | collective-permute-done | bytes 8224 | tf_op jit(solution)/shard_map/while/body/eval_jaxpr/ppermute | solution.py:10
  (199 shorter events, 60.9 us)
Async XLA Ops:
  7.2 64.8 %copy-start = (bf16[3,3,3,256,128]{4,3,2,1,0:T(8,128)(2,1)S(1)}, bf16[3,3,3,256,128]{4,3,2,1,0:T(8,128)(2,1)}, u32[]{:S(2)}) copy-start(bf16[3,3,3,256,128]{4,3,2,1,0:T(8,128)(2,1)} %param.43) | copy-start | bytes 5308420
  7.2 162.1 %reduce-scatter.10.cloned.1.call-start = ((), (), s32[]{:S(2)}) async-start(), calls=%async_computation.3 | async-start | bytes 786432
  8.0 6.5 %collective-permute-start = (bf16[16,128]{1,0:T(8,128)(2,1)S(1)}, bf16[16,128]{1,0:T(8,128)(2,1)S(1)}, u32[]{:S(2)}, u32[]{:S(2)}) collective-permute-start(bf16[16,128]{1,0:T(8,128)(2,1)S(1)} %get-tuple-element.324), channel_id=1, source_target_pairs={{2,0},{4,2},{6,4},{8,6},{10,8},{12,10},{14,12},{16,14},{18,16},{20... | collective-permute-start | bytes 12296 | tf_op jit(solution)/shard_map/while/body/eval_jaxpr/ppermute | solution.py:10
  14.5 11.2 %collective-permute-start = (bf16[16,128]{1,0:T(8,128)(2,1)S(1)}, bf16[16,128]{1,0:T(8,128)(2,1)S(1)}, u32[]{:S(2)}, u32[]{:S(2)}) collective-permute-start(bf16[16,128]{1,0:T(8,128)(2,1)S(1)} %get-tuple-element.324), channel_id=1, source_target_pairs={{2,0},{4,2},{6,4},{8,6},{10,8},{12,10},{14,12},{16,14},{18,16},{20... | collective-permute-start | bytes 12296 | tf_op jit(solution)/shard_map/while/body/eval_jaxpr/ppermute | solution.py:10
  25.8 11.2 %collective-permute-start = (bf16[16,128]{1,0:T(8,128)(2,1)S(1)}, bf16[16,128]{1,0:T(8,128)(2,1)S(1)}, u32[]{:S(2)}, u32[]{:S(2)}) collective-permute-start(bf16[16,128]{1,0:T(8,128)(2,1)S(1)} %get-tuple-element.324), channel_id=1, source_target_pairs={{2,0},{4,2},{6,4},{8,6},{10,8},{12,10},{14,12},{16,14},{18,16},{20... | collective-permute-start | bytes 12296 | tf_op jit(solution)/shard_map/while/body/eval_jaxpr/ppermute | solution.py:10
  37.0 11.2 %collective-permute-start = (bf16[16,128]{1,0:T(8,128)(2,1)S(1)}, bf16[16,128]{1,0:T(8,128)(2,1)S(1)}, u32[]{:S(2)}, u32[]{:S(2)}) collective-permute-start(bf16[16,128]{1,0:T(8,128)(2,1)S(1)} %get-tuple-element.324), channel_id=1, source_target_pairs={{2,0},{4,2},{6,4},{8,6},{10,8},{12,10},{14,12},{16,14},{18,16},{20... | collective-permute-start | bytes 12296 | tf_op jit(solution)/shard_map/while/body/eval_jaxpr/ppermute | solution.py:10
  50.7 12.0 %collective-permute-start.2 = (bf16[1,64,128]{2,1,0:T(8,128)(2,1)S(1)}, bf16[1,64,128]{2,1,0:T(8,128)(2,1)S(1)}, u32[]{:S(2)}, u32[]{:S(2)}) collective-permute-start(bf16[1,64,128]{2,1,0:T(8,128)(2,1)S(1)} %get-tuple-element.246), channel_id=1, source_target_pairs={{0,2},{2,4},{4,6},{6,8},{8,10},{10,12},{12,14},{14,16},{16,18},{18... | collective-permute-start | bytes 49160 | tf_op jit(solution)/shard_map/ppermute | solution.py:20
  52.7 11.5 %collective-permute-start.3 = (bf16[1,64,128]{2,1,0:T(8,128)(2,1)S(1)}, bf16[1,64,128]{2,1,0:T(8,128)(2,1)S(1)}, u32[]{:S(2)}, u32[]{:S(2)}) collective-permute-start(bf16[1,64,128]{2,1,0:T(8,128)(2,1)S(1)} %get-tuple-element.248), channel_id=1, source_target_pairs={{2,0},{4,2},{6,4},{8,6},{10,8},{12,10},{14,12},{16,14},{18,16},{20... | collective-permute-start | bytes 49160 | tf_op jit(solution)/shard_map/ppermute | solution.py:21
  75.6 11.9 %collective-permute-start.4 = (bf16[2,64,128]{2,1,0:T(8,128)(2,1)S(1)}, bf16[2,64,128]{2,1,0:T(8,128)(2,1)S(1)}, u32[]{:S(2)}, u32[]{:S(2)}) collective-permute-start(bf16[2,64,128]{2,1,0:T(8,128)(2,1)S(1)} %get-tuple-element.259), channel_id=1, source_target_pairs={{0,2},{2,4},{4,6},{6,8},{8,10},{10,12},{12,14},{14,16},{16,18},{18... | collective-permute-start | bytes 98312 | tf_op jit(solution)/shard_map/ppermute | solution.py:20
  77.5 11.6 %collective-permute-start.5 = (bf16[2,64,128]{2,1,0:T(8,128)(2,1)S(1)}, bf16[2,64,128]{2,1,0:T(8,128)(2,1)S(1)}, u32[]{:S(2)}, u32[]{:S(2)}) collective-permute-start(bf16[2,64,128]{2,1,0:T(8,128)(2,1)S(1)} %get-tuple-element.260), channel_id=1, source_target_pairs={{2,0},{4,2},{6,4},{8,6},{10,8},{12,10},{14,12},{16,14},{18,16},{20... | collective-permute-start | bytes 98312 | tf_op jit(solution)/shard_map/ppermute | solution.py:21
  100.6 12.1 %collective-permute-start.6 = (bf16[4,64,128]{2,1,0:T(8,128)(2,1)S(1)}, bf16[4,64,128]{2,1,0:T(8,128)(2,1)S(1)}, u32[]{:S(2)}, u32[]{:S(2)}) collective-permute-start(bf16[4,64,128]{2,1,0:T(8,128)(2,1)S(1)} %get-tuple-element.257), channel_id=1, source_target_pairs={{0,2},{2,4},{4,6},{6,8},{8,10},{10,12},{12,14},{14,16},{16,18},{18... | collective-permute-start | bytes 196616 | tf_op jit(solution)/shard_map/ppermute | solution.py:20
  102.5 11.9 %collective-permute-start.7 = (bf16[4,64,128]{2,1,0:T(8,128)(2,1)S(1)}, bf16[4,64,128]{2,1,0:T(8,128)(2,1)S(1)}, u32[]{:S(2)}, u32[]{:S(2)}) collective-permute-start(bf16[4,64,128]{2,1,0:T(8,128)(2,1)S(1)} %get-tuple-element.258), channel_id=1, source_target_pairs={{2,0},{4,2},{6,4},{8,6},{10,8},{12,10},{14,12},{16,14},{18,16},{20... | collective-permute-start | bytes 196616 | tf_op jit(solution)/shard_map/ppermute | solution.py:21
  125.1 0.7 copy-start.3
  125.1 0.7 copy-start.4
  126.4 11.1 %collective-permute-start.9 = (bf16[4,64,128]{2,1,0:T(8,128)(2,1)S(1)}, bf16[4,64,128]{2,1,0:T(8,128)(2,1)S(1)}, u32[]{:S(2)}, u32[]{:S(2)}) collective-permute-start(bf16[4,64,128]{2,1,0:T(8,128)(2,1)S(1)} %get-tuple-element.256), channel_id=1, source_target_pairs={{2,0},{4,2},{6,4},{8,6},{10,8},{12,10},{14,12},{16,14},{18,16},{20... | collective-permute-start | bytes 196616 | tf_op jit(solution)/shard_map/ppermute | solution.py:21
  135.5 12.4 %collective-permute-start.8 = (bf16[4,64,128]{2,1,0:T(8,128)(2,1)S(1)}, bf16[4,64,128]{2,1,0:T(8,128)(2,1)S(1)}, u32[]{:S(2)}, u32[]{:S(2)}) collective-permute-start(bf16[4,64,128]{2,1,0:T(8,128)(2,1)S(1)} %get-tuple-element.255), channel_id=1, source_target_pairs={{0,2},{2,4},{4,6},{6,8},{8,10},{10,12},{12,14},{14,16},{16,18},{18... | collective-permute-start | bytes 196616 | tf_op jit(solution)/shard_map/ppermute | solution.py:20
  151.7 19.4 %copy-start.2 = (f32[16,64,128]{2,1,0:T(8,128)S(1)}, f32[16,64,128]{2,1,0:T(8,128)}, u32[]{:S(2)}) copy-start(f32[16,64,128]{2,1,0:T(8,128)} %get-tuple-element.280) | copy-start | bytes 1572868
  153.2 59.7 %reduce-scatter.12.cloned.1.call-start = ((), (), s32[]{:S(2)}) async-start(), calls=%async_computation.4 | async-start | bytes 786432
  171.4 8.8 %collective-permute-start.11 = (bf16[2,64,128]{2,1,0:T(8,128)(2,1)S(1)}, bf16[2,64,128]{2,1,0:T(8,128)(2,1)S(1)}, u32[]{:S(2)}, u32[]{:S(2)}) collective-permute-start(bf16[2,64,128]{2,1,0:T(8,128)(2,1)S(1)} %get-tuple-element.254), channel_id=1, source_target_pairs={{2,0},{4,2},{6,4},{8,6},{10,8},{12,10},{14,12},{16,14},{18,16},{20... | collective-permute-start | bytes 98312 | tf_op jit(solution)/shard_map/ppermute | solution.py:21
  178.3 11.6 %collective-permute-start.10 = (bf16[2,64,128]{2,1,0:T(8,128)(2,1)S(1)}, bf16[2,64,128]{2,1,0:T(8,128)(2,1)S(1)}, u32[]{:S(2)}, u32[]{:S(2)}) collective-permute-start(bf16[2,64,128]{2,1,0:T(8,128)(2,1)S(1)} %get-tuple-element.253), channel_id=1, source_target_pairs={{0,2},{2,4},{4,6},{6,8},{8,10},{10,12},{12,14},{14,16},{16,18},{18... | collective-permute-start | bytes 98312 | tf_op jit(solution)/shard_map/ppermute | solution.py:20
  197.1 17.7 %copy-start.1 = (f32[16,64,128]{2,1,0:T(8,128)S(1)}, f32[16,64,128]{2,1,0:T(8,128)}, u32[]{:S(2)}) copy-start(f32[16,64,128]{2,1,0:T(8,128)} %get-tuple-element.278) | copy-start | bytes 1572868
  197.1 57.5 %reduce-scatter.14.cloned.1.call-start = ((), (), s32[]{:S(2)}) async-start(), calls=%async_computation.5 | async-start | bytes 786432
  215.1 8.8 %collective-permute-start.13 = (bf16[1,64,128]{2,1,0:T(8,128)(2,1)S(1)}, bf16[1,64,128]{2,1,0:T(8,128)(2,1)S(1)}, u32[]{:S(2)}, u32[]{:S(2)}) collective-permute-start(bf16[1,64,128]{2,1,0:T(8,128)(2,1)S(1)} %get-tuple-element.252), channel_id=1, source_target_pairs={{2,0},{4,2},{6,4},{8,6},{10,8},{12,10},{14,12},{16,14},{18,16},{20... | collective-permute-start | bytes 49160 | tf_op jit(solution)/shard_map/ppermute | solution.py:21
  221.9 11.4 %collective-permute-start.12 = (bf16[1,64,128]{2,1,0:T(8,128)(2,1)S(1)}, bf16[1,64,128]{2,1,0:T(8,128)(2,1)S(1)}, u32[]{:S(2)}, u32[]{:S(2)}) collective-permute-start(bf16[1,64,128]{2,1,0:T(8,128)(2,1)S(1)} %get-tuple-element.251), channel_id=1, source_target_pairs={{0,2},{2,4},{4,6},{6,8},{8,10},{10,12},{12,14},{14,16},{16,18},{18... | collective-permute-start | bytes 49160 | tf_op jit(solution)/shard_map/ppermute | solution.py:20
  261.4 11.3 %collective-permute-start.1 = (f32[16,128]{1,0:T(8,128)S(1)}, f32[16,128]{1,0:T(8,128)S(1)}, u32[]{:S(2)}, u32[]{:S(2)}) collective-permute-start(f32[16,128]{1,0:T(8,128)S(1)} %bitcast_add_fusion.2), channel_id=1, source_target_pairs={{0,2},{2,4},{4,6},{6,8},{8,10},{10,12},{12,14},{14,16},{16,18},{18... | collective-permute-start | bytes 24584 | tf_op jit(solution)/shard_map/while/body/eval_jaxpr/ppermute | solution.py:10
  272.7 11.3 %collective-permute-start.1 = (f32[16,128]{1,0:T(8,128)S(1)}, f32[16,128]{1,0:T(8,128)S(1)}, u32[]{:S(2)}, u32[]{:S(2)}) collective-permute-start(f32[16,128]{1,0:T(8,128)S(1)} %bitcast_add_fusion.2), channel_id=1, source_target_pairs={{0,2},{2,4},{4,6},{6,8},{8,10},{10,12},{12,14},{14,16},{16,18},{18... | collective-permute-start | bytes 24584 | tf_op jit(solution)/shard_map/while/body/eval_jaxpr/ppermute | solution.py:10
  284.0 11.3 %collective-permute-start.1 = (f32[16,128]{1,0:T(8,128)S(1)}, f32[16,128]{1,0:T(8,128)S(1)}, u32[]{:S(2)}, u32[]{:S(2)}) collective-permute-start(f32[16,128]{1,0:T(8,128)S(1)} %bitcast_add_fusion.2), channel_id=1, source_target_pairs={{0,2},{2,4},{4,6},{6,8},{8,10},{10,12},{12,14},{14,16},{16,18},{18... | collective-permute-start | bytes 24584 | tf_op jit(solution)/shard_map/while/body/eval_jaxpr/ppermute | solution.py:10
  295.3 11.3 %collective-permute-start.1 = (f32[16,128]{1,0:T(8,128)S(1)}, f32[16,128]{1,0:T(8,128)S(1)}, u32[]{:S(2)}, u32[]{:S(2)}) collective-permute-start(f32[16,128]{1,0:T(8,128)S(1)} %bitcast_add_fusion.2), channel_id=1, source_target_pairs={{0,2},{2,4},{4,6},{6,8},{8,10},{10,12},{12,14},{14,16},{16,18},{18... | collective-permute-start | bytes 24584 | tf_op jit(solution)/shard_map/while/body/eval_jaxpr/ppermute | solution.py:10
Sparse Core Ops, SparseCore 0:
  153.4 15.9 reduce-scatter.9
  197.2 15.6 reduce-scatter.11
  238.8 15.6 reduce-scatter.13
where the time goes:
time: 315 us; the launch traced here: 314 us
  waiting for transfers between devices  119 us (38%)
  starting transfers between devices  107 us (34%)
  blocking collectives  29.6 us (9%)
  matrix products  19.1 us (6%)
  local copies, waits for them, and re-layouts  18.9 us (6%)
  between operations  14.8 us (5%)
  other arithmetic  5.29 us (2%)
    ppermute x6, starting transfers between devices, padded_2(): after = lax.ppermute(initial, axis, down)  52.8 us
    ppermute x8, waiting for transfers between devices, passed_along(): lax.ppermute(value, axis, [(source, source + steps) for source in range(i...  42.7 us
    ppermute x8, starting transfers between devices, passed_along(): lax.ppermute(value, axis, [(source, source + steps) for source in range(i...  42.6 us
    unnamed x6, waiting for transfers between devices  42 us
    ppermute x6, waiting for transfers between devices, padded_2(): before = lax.ppermute(last, axis, up)  29.7 us
    all_gather x3, blocking collectives, local(): full = lax.all_gather(rimmed, 'chan', axis=2, tiled=True)  24 us
    unnamed x26, local copies, waits for them, and re-layouts  15 us
    ppermute x6, starting transfers between devices, padded_2(): before = lax.ppermute(last, axis, up)  11.5 us
  transfers between devices with their start and end apart: 23, of which 18 were waited for; matrix products, arithmetic and copies ran while one was open for 0% of the time, Pallas kernels for 0%

commit v1 on v0

v1 whole, which is shorter than its diff:
```python
import jax
import jax.numpy as jnp
from jax import lax
from jax.experimental import pallas as pl
from jax.experimental.pallas import tpu as pltpu
from jax.sharding import Mesh, PartitionSpec as P

BF = jnp.bfloat16
F32 = jnp.float32
CHROM = ("h", "yh", "yl", "core")
GROUP = ("yl", "core", "chan")
ALL = CHROM + ("chan",)
BAND = 64
C = 256
HALF = 128
OWN = 8
NT = (((1,), (1,)), ((), ()))


def dot(x, y):
    return jnp.dot(x, y, preferred_element_type=F32)


def dot_nt(x, y):
    return lax.dot_general(x, y, NT, preferred_element_type=F32)


def shifted(x, by):
    n = x.shape[0]
    if by > 0:
        return jnp.concatenate([x[by:], jnp.zeros((by, x.shape[1]), x.dtype)], axis=0)
    return jnp.concatenate([jnp.zeros((-by, x.shape[1]), x.dtype), x[: n + by]], axis=0)


def put(ref, row, x, r, sign):
    ref[row, :, 0:C] = shifted(x, -sign * r).astype(BF)
    ref[row, :, C : 2 * C] = x.astype(BF)
    ref[row, :, 2 * C : 3 * C] = shifted(x, sign * r).astype(BF)


def silu_parts(z):
    h = 0.5 * z
    t = jnp.tanh(h)
    return t, h + h * t


def slope(t, silu):
    s = 0.5 + 0.5 * t
    return s + silu * (0.5 - 0.5 * t)


def body(
    info, msg, w_own, w_z, w_s, out,
    w, lcan, rcan, ccan, lwin, rwin, u_all, v_all, e0, e63,
    pp1, pp2, pd2, pd1, ds0, ds1, g2, p3, d0, g1h, g1l, rcv, lcv, ccv, sem,
):
    q, first, core, chan, total = info[0], info[1], info[2], info[3], info[4]
    mine = pl.ds(pl.multiple_of(chan * HALF, HALF), HALF)
    theirs = pl.ds(pl.multiple_of((1 - chan) * HALF, HALF), HALF)
    near = pl.ds(pl.multiple_of(core * HALF, HALF), HALF)
    far = pl.ds(pl.multiple_of((1 - core) * HALF, HALF), HALF)
    copies = []
    for k in range(3):
        taps = pl.ds(9 * k, 9)
        copies.append([
            pltpu.make_async_copy(w_own.at[taps], w.at[taps, :, mine], sem.at[k, 0]),
            pltpu.make_async_copy(w_z.at[taps], w.at[taps, near, theirs], sem.at[k, 1]),
            pltpu.make_async_copy(w_s.at[taps], w.at[taps, far, theirs], sem.at[k, 2]),
        ])
        for c in copies[k]:
            c.start()

    def valid(row):
        i = first + row
        return jnp.where((i >= 0) & (i < total), 1.0, 0.0).astype(F32)

    lcan[160:176] = jnp.zeros((16, C), F32)
    rcan[160:176] = jnp.zeros((16, C), F32)
    ccan[160:192] = jnp.zeros((32, HALF), F32)
    for j in range(4):
        for g in range(2):
            e = 2 * j + g
            lanes = slice(HALF * g, HALF * g + HALF)
            places = [(16, 16 + 16 * j), (64, 80 + 16 * j)]
            if j == 0:
                places.append((112, 0))
            if j == 3:
                places.append((112, 144))
            for at, to in places:
                lcan[to : to + 16, lanes] = msg[e, at : at + 16].astype(F32)
                rcan[to : to + 16, lanes] = msg[e, at + 16 : at + 32].astype(F32)
                cot = msg[e, at + 32 : at + 48].astype(F32)
                if g == 0:
                    ccan[to : to + 16] = cot
                else:
                    ccan[to : to + 16] = ccan[to : to + 16] + cot
    read3 = jnp.concatenate([msg[0, 0:16], msg[1, 0:16]], axis=1).astype(F32)
    readout = jnp.sum(read3, axis=0, keepdims=True)
    start = pl.multiple_of(q * OWN, OWN)
    lwin[...] = lcan[pl.ds(start, 48)]
    rwin[...] = rcan[pl.ds(start, 112)]
    cot_t = jnp.transpose(ccan[pl.ds(pl.multiple_of(start + 8, OWN), 128)])

    for c in copies[0]:
        c.wait()
    ul, va, vb = [None] * 3, [None] * 3, [None] * 3
    for b in range(3):
        for a in range(3):
            lhs = jnp.concatenate([lwin[2 + a : 42 + a], rwin[1 + a + b : 105 + a + b]], axis=0)
            y = dot(lhs.astype(BF), w[3 * a + b])
            ul[b] = y[:40] if a == 0 else ul[b] + y[:40]
            if a == 0:
                va[b] = y[40:]
            else:
                vb[b] = y[40:] if a == 1 else vb[b] + y[40:]
    u_all[...] = ul[0] + ul[1] + ul[2]
    for var in range(2):
        v = [vb[b] + va[b] if var == 0 else vb[b] for b in range(3)]
        v_all[var] = v[0] + v[1] + v[2]
        e0[var] = ul[1] + ul[2] + (v[1] + v[2])[:40]
        e63[var] = ul[0] + ul[1] + (v[0] + v[1])[63:103]
    diag = lax.broadcasted_iota(jnp.int32, (BAND, C), 0)
    for t in range(34):
        row = t - 13
        var = jnp.where(first + row == 0, 1, 0)
        pair = (lwin[t + 3 : t + 4] + rwin[t + 3 : t + 67]).astype(BF).astype(F32)
        pre = u_all[t : t + 1] + v_all[var, t : t + BAND]
        pre = jnp.where(diag == 0, e0[var, t : t + 1], pre)
        pre = jnp.where(diag == BAND - 1, e63[var, t : t + 1], pre)
        th, sil = silu_parts(pre)
        if 12 <= t < 22:
            ds0[t - 12] = slope(th, sil).astype(BF)
        put(pp1, t, (pair + sil) * valid(row), 2, 1)

    for c in copies[1]:
        c.wait()
    n = 5
    for t0 in range(0, 30, n):
        acc = None
        for a in range(3):
            x = pp1[t0 + 2 * a : t0 + 2 * a + n].reshape(n * BAND, 3 * C)
            y = dot(x, w[9 + 3 * a : 12 + 3 * a].reshape(3 * C, C))
            acc = y if acc is None else acc + y
        for s in range(n):
            t = t0 + s
            th, sil = silu_parts(acc[s * BAND : (s + 1) * BAND])
            if 8 <= t < 22:
                ds1[t - 8] = slope(th, sil).astype(BF)
            pair = pp1[t + 2, :, C : 2 * C].astype(F32)
            put(pp2, t, (pair + sil) * valid(t - 11), 4, 1)

    for c in copies[2]:
        c.wait()

    def top(row):
        return cot_t[:BAND, row + 8 : row + 9] * readout

    n = 11
    for t0 in range(0, 22, n):
        acc = None
        for a in range(3):
            x = pp2[t0 + 4 * a : t0 + 4 * a + n].reshape(n * BAND, 3 * C)
            y = dot(x, w[18 + 3 * a : 21 + 3 * a].reshape(3 * C, C))
            acc = y if acc is None else acc + y
        for s in range(n):
            t = t0 + s
            th, sil = silu_parts(acc[s * BAND : (s + 1) * BAND])
            if 7 <= t < 15:
                p3[t - 7] = (pp2[t + 4, :, C : 2 * C].astype(F32) + sil).astype(BF)
            put(pd2, t, top(t - 7) * slope(th, sil), 4, -1)
    ccv[...] = jnp.zeros((64, HALF), F32)
    read_b = read3.astype(BF)
    rows = [jnp.sum(dot_nt(read_b, p3[s]), axis=0, keepdims=True) for s in range(OWN)]
    ccv[pl.ds(start, OWN), :BAND] = jnp.concatenate(rows, axis=0)

    n = 7
    for t0 in range(0, 14, n):
        acc = None
        for a in range(3):
            x = pd2[t0 + 8 - 4 * a : t0 + 8 - 4 * a + n].reshape(n * BAND, 3 * C)
            for b in range(3):
                y = dot_nt(x[:, b * C : (b + 1) * C], w[18 + 3 * a + b])
                acc = y if acc is None else acc + y
        for s in range(n):
            t = t0 + s
            grad = top(t - 3) + acc[s * BAND : (s + 1) * BAND]
            if 2 <= t < 12:
                g2[t - 2] = grad
            put(pd1, t, grad * ds1[t].astype(F32) * valid(t - 3), 2, -1)

    n = 5
    for t0 in range(0, 10, n):
        acc = None
        for a in range(3):
            x = pd1[t0 + 4 - 2 * a : t0 + 4 - 2 * a + n].reshape(n * BAND, 3 * C)
            for b in range(3):
                y = dot_nt(x[:, b * C : (b + 1) * C], w[9 + 3 * a + b])
                acc = y if acc is None else acc + y
        for s in range(n):
            t = t0 + s
            grad = g2[t] + acc[s * BAND : (s + 1) * BAND]
            if 1 <= t < 9:
                hi = grad.astype(BF)
                g1h[t - 1] = hi
                g1l[t - 1] = (grad - hi.astype(F32)).astype(BF)
            d0[t] = (grad * ds0[t].astype(F32) * valid(t - 1)).astype(BF)

    def chooser(rows_in, a, b):
        shape = (80, rows_in * BAND)
        to = lax.broadcasted_iota(jnp.int32, shape, 0)
        at = lax.broadcasted_iota(jnp.int32, shape, 1)
        i = (at >> 6) + a
        d = (at & 63) + b
        inside = (i >= 0) & (i < OWN) & (d >= 0) & (d < BAND)
        hit = ((to < 72) & (i + d == to)) | ((to >= 72) & (i == to - 72))
        return jnp.where(inside & hit, 1.0, 0.0).astype(BF)

    own = chooser(OWN, 0, 0)
    total80 = dot(own, g1h[...].reshape(OWN * BAND, C)) + dot(own, g1l[...].reshape(OWN * BAND, C))
    dd = d0[...].reshape(10 * BAND, C)
    for a in range(3):
        for b in range(3):
            z = dot(chooser(10, a - 2, b - 1), dd)
            total80 = total80 + dot_nt(z.astype(BF), w[3 * a + b])
    rcv[...] = jnp.zeros((128, C), F32)
    lcv[...] = jnp.zeros((64, C), F32)
    rcv[pl.ds(start, 72)] = total80[:72]
    lcv[pl.ds(start, OWN)] = total80[72:]
    for j in range(4):
        for g in range(2):
            lanes = slice(HALF * g, HALF * g + HALF)
            out[2 * j + g, 0:16] = rcv[16 * j : 16 * j + 16, lanes]
            out[2 * j + g, 16:32] = rcv[64 + 16 * j : 80 + 16 * j, lanes]
            out[2 * j + g, 32:48] = lcv[16 * j : 16 * j + 16, lanes]
            out[2 * j + g, 48:64] = ccv[16 * j : 16 * j + 16]


def local_part(info, msg, w_own, w_z, w_s):
    vm = pltpu.VMEM
    scratch = [
        vm((27, C, C), BF),
        vm((176, C), F32),
        vm((176, C), F32),
        vm((192, HALF), F32),
        vm((48, C), F32),
        vm((112, C), F32),
        vm((40, C), F32),
        vm((2, 104, C), F32),
        vm((2, 40, C), F32),
        vm((2, 40, C), F32),
        vm((34, BAND, 3 * C), BF),
        vm((30, BAND, 3 * C), BF),
        vm((22, BAND, 3 * C), BF),
        vm((14, BAND, 3 * C), BF),
        vm((10, BAND, C), BF),
        vm((14, BAND, C), BF),
        vm((10, BAND, C), F32),
        vm((8, BAND, C), BF),
        vm((10, BAND, C), BF),
        vm((8, BAND, C), BF),
        vm((8, BAND, C), BF),
        vm((128, C), F32),
        vm((64, C), F32),
        vm((64, HALF), F32),
        pltpu.SemaphoreType.DMA((3, 3)),
    ]
    return pl.pallas_call(
        body,
        out_shape=jax.ShapeDtypeStruct((8, 64, HALF), F32),
        in_specs=[
            pl.BlockSpec(memory_space=pltpu.SMEM),
            pl.BlockSpec(memory_space=vm),
            pl.BlockSpec(memory_space=pl.ANY),
            pl.BlockSpec(memory_space=pl.ANY),
            pl.BlockSpec(memory_space=pl.ANY),
        ],
        out_specs=pl.BlockSpec(memory_space=vm),
        scratch_shapes=scratch,
        compiler_params=pltpu.CompilerParams(vmem_limit_bytes=48 * 2**20),
        cost_estimate=pl.CostEstimate(
            flops=6 * 10**9, bytes_accessed=5 * 10**6, transcendentals=2 * 10**6
        ),
        name="decoder",
    )(info, msg, w_own, w_z, w_s)


def flat(h, yh, yl, core, chan):
    return (((h * 4 + yh) * 2 + yl) * 2 + core) * 2 + chan


def z_pairs(chroms):
    pairs = []
    per_z = chroms // 4
    for ch in range(chroms):
        step = 1 if ch % 2 == 0 else -1
        hi, rest = ch // per_z, ch % per_z
        for g in range(2):
            z = (2 * hi + g + step) % 8
            pairs.append((((z // 2) * per_z + rest) * 2 + z % 2, 2 * ch + g))
    return pairs


def parts_of(x, count):
    parts = []
    for _ in range(count):
        hi = lax.reduce_precision(x, 8, 7)
        parts.append(hi.astype(BF))
        x = x - hi
    return parts


def local(left, right, weight, readout, cotangent):
    rows = left.shape[0]
    chroms = lax.axis_size(CHROM)
    slab = lax.axis_index(CHROM)
    core = lax.axis_index("core")
    chan = lax.axis_index("chan")
    own_w = weight.reshape(27, C, HALF)
    piece = lax.dynamic_slice_in_dim(own_w, core * HALF, HALF, axis=1)
    w_z = lax.ppermute(piece, ALL, z_pairs(chroms))

    hi, lo = parts_of(cotangent, 2)
    cot = jnp.pad(jnp.where(chan == 0, hi, lo), ((0, 0), (0, HALF - BAND)))
    mine = jnp.concatenate([left, right, cot], axis=0)
    slabs = 4
    groups = chroms // slabs
    next_group = [
        (slabs * (g + 1) + j, slabs * g + j) for g in range(groups - 1) for j in range(slabs)
    ]
    ends = [(slabs * g + 3, slabs * (g + 1)) for g in range(groups - 1)]
    ends += [(slabs * (g + 2), slabs * g + 3) for g in range(groups - 2)]
    after = lax.ppermute(mine, CHROM, next_group)
    edge = lax.ppermute(mine, CHROM, ends)
    read = jnp.pad(jnp.stack(parts_of(readout, 3)), ((0, 13), (0, 0)))
    block = jnp.concatenate([read, mine, after, edge], axis=0)
    msg = lax.all_to_all(
        jnp.broadcast_to(block[None], (8,) + block.shape), GROUP, 0, 0, tiled=False
    )
    w_s = lax.ppermute(w_z, "core", [(0, 1), (1, 0)])
    q = lax.axis_index(GROUP)
    info = jnp.stack(
        [q, rows * slab + OWN * chan, core, chan, rows * chroms]
    ).astype(jnp.int32)
    sent = local_part(info, msg, own_w, w_z, w_s)
    got = jnp.sum(lax.all_to_all(sent, GROUP, 0, 0, tiled=False), axis=0)
    moved = lax.ppermute(got[16:32], CHROM, [(b, a) for a, b in next_group])
    return got[48:64, :BAND], got[32:48], got[0:16] + moved


def solution(mesh):
    chroms = mesh.shape["chrom"]
    small = Mesh(
        mesh.devices.reshape(chroms // 16, 4, 2, 2, 2), ("h", "yh", "yl", "core", "chan")
    )
    return jax.shard_map(
        local,
        mesh=small,
        in_specs=(
            P(CHROM, "chan"),
            P(CHROM, "chan"),
            P(None, None, None, None, "chan"),
            P("chan"),
            P(CHROM, None),
        ),
        out_specs=(P(CHROM, None), P(CHROM, "chan"), P(CHROM, "chan")),
        check_vma=False,
    )
```

time: 315 us -> 88.7 us (0.28)
  the two profiles are of different devices: /device:TPU:256 before, /device:TPU:128 now
where the time goes in v1:
time: 88.7 us; the launch traced here: 88.3 us
  waiting for transfers between devices  35.5 us (40%)
  starting transfers between devices  25.8 us (29%)
  Pallas kernels  13.2 us (15%)
  blocking collectives  8.57 us (10%)
  local copies, waits for them, and re-layouts  3.84 us (4%)
    ppermute x1, waiting for transfers between devices, local(): w_z = lax.ppermute(piece, ALL, z_pairs(chroms))  13.4 us
    pallas_call x1, Pallas kernels, local_part(): pl.pallas_call(body, out_shape=jax.ShapeDtypeStruct((8, 64, HALF), F32),...  13.2 us
    ppermute x1, starting transfers between devices, local(): after = lax.ppermute(mine, CHROM, next_group)  12.8 us
    ppermute x1, waiting for transfers between devices, local(): moved = lax.ppermute(got[16:32], CHROM, [(b, a) for a, b in next_group])  9.12 us
    all_to_all x1, blocking collectives, local(): got = jnp.sum(lax.all_to_all(sent, GROUP, 0, 0, tiled=False), axis=0)  8.57 us
    all_to_all x1, waiting for transfers between devices, local(): lax.all_to_all(jnp.broadcast_to(block[None], (8,) + block.shape), GROUP,...  6.55 us
    ppermute x1, waiting for transfers between devices, local(): edge = lax.ppermute(mine, CHROM, ends)  6.35 us
    ppermute x1, starting transfers between devices, local(): edge = lax.ppermute(mine, CHROM, ends)  3.75 us
  transfers between devices with their start and end apart: 6, of which 4 were waited for; matrix products, arithmetic and copies ran while one was open for 2% of the time, Pallas kernels for 0%

profile of v1, /device:TPU:128, one launch (start us, length us, event | category | flops | bytes accessed | tf_op | source)
XLA Modules:
  0.0 88.3 jit_solution(13754456712391777270)
XLA Ops:
  0.6 0.0 copy-start
  0.6 0.0 copy-start.4
  0.7 0.0 copy-start.1
  0.7 0.0 copy-start.2
  0.7 0.0 copy-start.3
  0.7 2.3 %constant_dynamic-slice_fusion = bf16[27,128,128]{2,1,0:T(8,128)(2,1)} fusion(bf16[27,256,128]{2,1,0:T(8,128)(2,1)} %bitcast.11, s32[]{:T(128)S(6)} %select_n.13), kind=kLoop, calls=%fused_computation.28 | loop fusion | bytes 1769476 | tf_op jit(solution)/shard_map/dynamic_slice | solution.py:319
  3.0 1.9 %collective-permute-start.2 = (bf16[27,128,128]{2,1,0:T(8,128)(2,1)}, bf16[27,128,128]{2,1,0:T(8,128)(2,1)S(1)}, u32[]{:S(2)}, u32[]{:S(2)}) collective-permute-start(bf16[27,128,128]{2,1,0:T(8,128)(2,1)} %constant_dynamic-slice_fusion), channel_id=1, source_target_pairs={{1,0},{128,1},{387,2},{2,3},{5,4},{132,5},{391,6},{6,7},{9,8},{136... | collective-permute-start | bytes 2654216 | tf_op jit(solution)/shard_map/ppermute | solution.py:320
  4.9 0.0 copy-done.4
  5.0 0.0 copy-done.1
  5.0 0.0 copy-done.2
  5.0 0.0 copy-done.3
  5.0 13.4 %collective-permute-done.2.w_z = bf16[27,128,128]{2,1,0:T(8,128)(2,1)S(1)} collective-permute-done((bf16[27,128,128]{2,1,0:T(8,128)(2,1)}, bf16[27,128,128]{2,1,0:T(8,128)(2,1)S(1)}, u32[]{:S(2)}, u32[]{:S(2)}) %collective-permute-start.2) | collective-permute-done | bytes 884768 | tf_op jit(solution)/shard_map/ppermute | solution.py:320
  18.5 1.9 %collective-permute-start.3 = (bf16[27,128,128]{2,1,0:T(8,128)(2,1)S(1)}, bf16[27,128,128]{2,1,0:T(8,128)(2,1)}, u32[]{:S(2)}, u32[]{:S(2)}) collective-permute-start(bf16[27,128,128]{2,1,0:T(8,128)(2,1)S(1)} %collective-permute-done.2.w_z), channel_id=1, source_target_pairs={{0,2},{2,0},{1,3},{3,1},{4,6},{6,4},{5,7},{7,5},{8,10},{10,8},{9,1... | collective-permute-start | bytes 2654216 | tf_op jit(solution)/shard_map/ppermute | solution.py:339
  20.4 12.8 %collective-permute-start = (bf16[48,128]{1,0:T(8,128)(2,1)S(1)}, bf16[48,128]{1,0:T(8,128)(2,1)S(1)}, u32[]{:S(2)}, u32[]{:S(2)}) collective-permute-start(bf16[48,128]{1,0:T(8,128)(2,1)S(1)} %pad_maximum_fusion), channel_id=1, source_target_pairs={{8,0},{10,2},{12,4},{14,6},{16,8},{18,10},{20,12},{22,14},{24,16},... | collective-permute-start | bytes 36872 | tf_op jit(solution)/shard_map/ppermute | solution.py:332
  33.3 3.8 %collective-permute-start.1 = (bf16[48,128]{1,0:T(8,128)(2,1)S(1)}, bf16[48,128]{1,0:T(8,128)(2,1)S(1)}, u32[]{:S(2)}, u32[]{:S(2)}) collective-permute-start(bf16[48,128]{1,0:T(8,128)(2,1)S(1)} %pad_maximum_fusion), channel_id=1, source_target_pairs={{6,8},{14,16},{22,24},{30,32},{38,40},{46,48},{54,56},{62,64},{70,... | collective-permute-start | bytes 36872 | tf_op jit(solution)/shard_map/ppermute | solution.py:333
  37.0 0.0 collective-permute-done
  37.1 6.3 %collective-permute-done.1 = bf16[48,128]{1,0:T(8,128)(2,1)S(1)} collective-permute-done((bf16[48,128]{1,0:T(8,128)(2,1)S(1)}, bf16[48,128]{1,0:T(8,128)(2,1)S(1)}, u32[]{:S(2)}, u32[]{:S(2)}) %collective-permute-start.1) | collective-permute-done | bytes 12320 | tf_op jit(solution)/shard_map/ppermute | solution.py:333
  43.4 0.8 broadcast_in_dim.2
  44.2 3.4 %all-to-all-start = ((bf16[8,160,128]{2,1,0:T(8,128)(2,1)}), bf16[8,160,128]{2,1,0:T(8,128)(2,1)S(1)}, u32[]{:S(2)}, u32[]{:S(2)}) async-start(bf16[8,160,128]{2,1,0:T(8,128)(2,1)} %broadcast_in_dim.2), calls=%async_computation | async-start | bytes 655360 | tf_op jit(solution)/shard_map/all_to_all | solution.py:336
  47.6 0.1 stack.31.info
  47.7 6.6 %all-to-all-done.msg = bf16[8,160,128]{2,1,0:T(8,128)(2,1)S(1)} async-done(((bf16[8,160,128]{2,1,0:T(8,128)(2,1)}), bf16[8,160,128]{2,1,0:T(8,128)(2,1)S(1)}, u32[]{:S(2)}, u32[]{:S(2)}) %all-to-all-start) | async-done | bytes 327712 | tf_op jit(solution)/shard_map/all_to_all | solution.py:336
  54.3 0.0 collective-permute-done.3.w_s
  54.3 0.0 copy-done
  54.3 13.2 %decoder.1 = f32[8,64,128]{2,1,0:T(8,128)S(1)} custom-call(s32[5]{0:T(128)S(1)} %stack.31.info, bf16[8,160,128]{2,1,0:T(8,128)(2,1)S(1)} %all-to-all-done.msg, bf16[27,256,128]{2,1,0:T(8,128)(2,1)S(1)} %bitcast.12, bf16[27,128,128]{2,1,0:T(8,128)(2,1)S(1)} %collective-permute-done.2.w_z, bf16[27,128,128]{2,1,0:T(8,128)(2,1)} %collective-permute-done.3.w_s), custom_call_target="tpu_custom_call" | custom-call | flops 6000000000 | bytes 5000000 | tf_op jit(solution)/shard_map/decoder/pallas_call | solution.py:267
  67.5 8.6 %all_to_all.10 = f32[8,64,128]{2,1,0:T(8,128)S(1)} all-to-all(f32[8,64,128]{2,1,0:T(8,128)S(1)} %decoder.1), channel_id=1, replica_groups=mesh['h'=16,'yh'=4,'yl'=2,'core'=2,'chan'=2] {'yl','core','chan'}, dimensions={0} | all-to-all | bytes 524288 | tf_op jit(solution)/shard_map/all_to_all | solution.py:345
  76.1 1.9 %collective-permute-start.4 = (f32[16,128]{1,0:T(8,128)S(1)}, f32[16,128]{1,0:T(8,128)S(1)}, u32[]{:S(2)}, u32[]{:S(2)}) collective-permute-start(f32[16,128]{1,0:T(8,128)S(1)} %slice.19), channel_id=1, source_target_pairs={{0,8},{2,10},{4,12},{6,14},{8,16},{10,18},{12,20},{14,22},{16,24},... | collective-permute-start | bytes 24584 | tf_op jit(solution)/shard_map/ppermute | solution.py:346
  78.0 0.6 slice.16
  78.6 9.1 %collective-permute-done.4 = f32[16,128]{1,0:T(8,128)S(1)} collective-permute-done((f32[16,128]{1,0:T(8,128)S(1)}, f32[16,128]{1,0:T(8,128)S(1)}, u32[]{:S(2)}, u32[]{:S(2)}) %collective-permute-start.4) | collective-permute-done | bytes 8224 | tf_op jit(solution)/shard_map/ppermute | solution.py:346
  87.7 0.6 slice_add_fusion
  (11 shorter events, 0.1 us)
Async XLA Ops:
  0.6 53.7 %copy-start = (bf16[3,3,3,256,128]{4,3,2,1,0:T(8,128)(2,1)S(1)}, bf16[3,3,3,256,128]{4,3,2,1,0:T(8,128)(2,1)}, u32[]{:S(2)}) copy-start(bf16[3,3,3,256,128]{4,3,2,1,0:T(8,128)(2,1)} %param.7) | copy-start | bytes 5308420
  0.6 4.3 %copy-start.4 = (f32[128]{0:T(128)S(1)}, f32[128]{0:T(128)}, u32[]{:S(2)}) copy-start(f32[128]{0:T(128)} %param.8) | copy-start | bytes 1540
  0.7 4.3 %copy-start.1 = (bf16[16,128]{1,0:T(8,128)(2,1)S(1)}, bf16[16,128]{1,0:T(8,128)(2,1)}, u32[]{:S(2)}) copy-start(bf16[16,128]{1,0:T(8,128)(2,1)} %param.5) | copy-start | bytes 12292
  0.7 4.3 %copy-start.2 = (bf16[16,128]{1,0:T(8,128)(2,1)S(1)}, bf16[16,128]{1,0:T(8,128)(2,1)}, u32[]{:S(2)}) copy-start(bf16[16,128]{1,0:T(8,128)(2,1)} %param.6) | copy-start | bytes 12292
  0.7 4.3 %copy-start.3 = (f32[16,64]{1,0:T(8,128)S(1)}, f32[16,64]{1,0:T(8,128)}, u32[]{:S(2)}) copy-start(f32[16,64]{1,0:T(8,128)} %param.9) | copy-start | bytes 12292
  3.0 15.5 %collective-permute-start.2 = (bf16[27,128,128]{2,1,0:T(8,128)(2,1)}, bf16[27,128,128]{2,1,0:T(8,128)(2,1)S(1)}, u32[]{:S(2)}, u32[]{:S(2)}) collective-permute-start(bf16[27,128,128]{2,1,0:T(8,128)(2,1)} %constant_dynamic-slice_fusion), channel_id=1, source_target_pairs={{1,0},{128,1},{387,2},{2,3},{5,4},{132,5},{391,6},{6,7},{9,8},{136... | collective-permute-start | bytes 2654216 | tf_op jit(solution)/shard_map/ppermute | solution.py:320
  18.5 35.8 %collective-permute-start.3 = (bf16[27,128,128]{2,1,0:T(8,128)(2,1)S(1)}, bf16[27,128,128]{2,1,0:T(8,128)(2,1)}, u32[]{:S(2)}, u32[]{:S(2)}) collective-permute-start(bf16[27,128,128]{2,1,0:T(8,128)(2,1)S(1)} %collective-permute-done.2.w_z), channel_id=1, source_target_pairs={{0,2},{2,0},{1,3},{3,1},{4,6},{6,4},{5,7},{7,5},{8,10},{10,8},{9,1... | collective-permute-start | bytes 2654216 | tf_op jit(solution)/shard_map/ppermute | solution.py:339
  20.4 16.6 %collective-permute-start = (bf16[48,128]{1,0:T(8,128)(2,1)S(1)}, bf16[48,128]{1,0:T(8,128)(2,1)S(1)}, u32[]{:S(2)}, u32[]{:S(2)}) collective-permute-start(bf16[48,128]{1,0:T(8,128)(2,1)S(1)} %pad_maximum_fusion), channel_id=1, source_target_pairs={{8,0},{10,2},{12,4},{14,6},{16,8},{18,10},{20,12},{22,14},{24,16},... | collective-permute-start | bytes 36872 | tf_op jit(solution)/shard_map/ppermute | solution.py:332
  33.3 10.1 %collective-permute-start.1 = (bf16[48,128]{1,0:T(8,128)(2,1)S(1)}, bf16[48,128]{1,0:T(8,128)(2,1)S(1)}, u32[]{:S(2)}, u32[]{:S(2)}) collective-permute-start(bf16[48,128]{1,0:T(8,128)(2,1)S(1)} %pad_maximum_fusion), channel_id=1, source_target_pairs={{6,8},{14,16},{22,24},{30,32},{38,40},{46,48},{54,56},{62,64},{70,... | collective-permute-start | bytes 36872 | tf_op jit(solution)/shard_map/ppermute | solution.py:333
  44.2 10.1 %all-to-all-start = ((bf16[8,160,128]{2,1,0:T(8,128)(2,1)}), bf16[8,160,128]{2,1,0:T(8,128)(2,1)S(1)}, u32[]{:S(2)}, u32[]{:S(2)}) async-start(bf16[8,160,128]{2,1,0:T(8,128)(2,1)} %broadcast_in_dim.2), calls=%async_computation | async-start | bytes 655360 | tf_op jit(solution)/shard_map/all_to_all | solution.py:336
  76.1 11.7 %collective-permute-start.4 = (f32[16,128]{1,0:T(8,128)S(1)}, f32[16,128]{1,0:T(8,128)S(1)}, u32[]{:S(2)}, u32[]{:S(2)}) collective-permute-start(f32[16,128]{1,0:T(8,128)S(1)} %slice.19), channel_id=1, source_target_pairs={{0,8},{2,10},{4,12},{6,14},{8,16},{10,18},{12,20},{14,22},{16,24},... | collective-permute-start | bytes 24584 | tf_op jit(solution)/shard_map/ppermute | solution.py:346

commit v2 on v1

v2 whole, which is shorter than its diff:
```python
import jax
import jax.numpy as jnp
from jax import lax
from jax.experimental import pallas as pl
from jax.experimental.pallas import tpu as pltpu
from jax.sharding import Mesh, PartitionSpec as P

BF = jnp.bfloat16
F32 = jnp.float32
CHROM = ("h", "yh", "yl", "core")
GROUP = ("yl", "core", "chan")
ALL = CHROM + ("chan",)
BAND = 64
C = 256
HALF = 128
OWN = 8
NT = (((1,), (1,)), ((), ()))


def dot(x, y):
    return jnp.dot(x, y, preferred_element_type=F32)


def dot_nt(x, y):
    return lax.dot_general(x, y, NT, preferred_element_type=F32)


def shifted(x, by):
    n = x.shape[0]
    if by > 0:
        return jnp.concatenate([x[by:], jnp.zeros((by, x.shape[1]), x.dtype)], axis=0)
    return jnp.concatenate([jnp.zeros((-by, x.shape[1]), x.dtype), x[: n + by]], axis=0)


def put(ref, row, x, r, sign):
    ref[row, :, 0:C] = shifted(x, -sign * r)
    ref[row, :, C : 2 * C] = x
    ref[row, :, 2 * C : 3 * C] = shifted(x, sign * r)


def gate(h):
    p = 1.0 + jnp.tanh(h)
    return p, h * p


def slope2(p, silu):
    return p + silu * (2.0 - p)


def spans(rows, n):
    return [(t, min(n, rows - t)) for t in range(0, rows, n)]


def side_by_side(w, tap):
    return jnp.concatenate([w[tap + k] for k in range(9)], axis=1)


def body(
    info, msg, w_own, w_z, w_s, out,
    w, lcan, rcan, ccan, lwin, rwin, u_all, v_all, e0, e63,
    pp1, pp2, pd2, pd1, ds0, ds1, g2, p3, d0, g1h, g1l, rcv, lcv, ccv, sem,
):
    q, first, core, chan, total = info[0], info[1], info[2], info[3], info[4]
    mine = pl.ds(pl.multiple_of(chan * HALF, HALF), HALF)
    theirs = pl.ds(pl.multiple_of((1 - chan) * HALF, HALF), HALF)
    near = pl.ds(core * 13, 14)
    far = pl.ds((1 - core) * 13, 14)
    first_copies = [
        pltpu.make_async_copy(w_z, w.at[near, :, theirs], sem.at[3]),
        pltpu.make_async_copy(w_s, w.at[far, :, theirs], sem.at[4]),
    ]
    copies = []
    for k in range(3):
        taps = pl.ds(9 * k, 9)
        copies.append(pltpu.make_async_copy(w_own.at[taps], w.at[taps, :, mine], sem.at[k]))
    first_copies.append(copies[0])
    for c in first_copies + copies[1:]:
        c.start()

    def valid(row):
        i = first + row
        return jnp.where((i >= 0) & (i < total), 1.0, 0.0)

    lcan[96:176] = jnp.zeros((80, C), F32)
    rcan[160:176] = jnp.zeros((16, C), F32)
    ccan[96:192] = jnp.zeros((96, HALF), F32)
    def place(ref, to, lanes, x):
        ref[to : to + 16, lanes] = x.astype(F32)

    for j in range(4):
        for g in range(2):
            e = 2 * j + g
            lanes = slice(HALF * g, HALF * g + HALF)
            place(lcan, 16 + 16 * j, lanes, msg[e, 0:16])
            place(rcan, 16 + 16 * j, lanes, msg[e, 16:32])
            place(rcan, 80 + 16 * j, lanes, msg[e, 48:64])
            if j == 0:
                place(lcan, 80, lanes, msg[e, 64:80])
            if j == 1:
                place(lcan, 0, lanes, msg[e, 64:80])
                place(rcan, 0, lanes, msg[e, 80:96])
            if j == 3:
                place(rcan, 144, lanes, msg[e, 80:96])
    for to, j, at in ((0, 1, 96), (16, 0, 32), (32, 1, 32), (48, 2, 32), (64, 3, 32), (80, 0, 96)):
        ccan[to : to + 16] = msg[2 * j, at : at + 16].astype(F32) + msg[2 * j + 1, at : at + 16].astype(F32)
    halves = []
    lane = lax.broadcasted_iota(jnp.int32, (1, HALF), 1)
    for g in range(2):
        m = msg[g, 32:48].astype(F32)
        even, odd = m[0:1] + m[2:3] + m[4:5], m[1:2] + m[3:4] + m[5:6]
        halves.append(jnp.where(lane < BAND, pltpu.roll(even, BAND, 1), odd))
    readout = jnp.concatenate(halves, axis=1)
    rest, parts = readout, []
    for _ in range(3):
        parts.append(rest.astype(BF).astype(F32))
        rest = rest - parts[-1]
    read_b = jnp.concatenate(parts + [jnp.zeros((13, C), F32)], axis=0).astype(BF)
    start = pl.multiple_of(q * OWN, OWN)
    lwin[...] = lcan[pl.ds(start, 48)]
    rwin[...] = rcan[pl.ds(start, 112)]
    cot_t = jnp.transpose(ccan[pl.ds(pl.multiple_of(start + 8, OWN), 128)])

    for c in first_copies:
        c.wait()
    ul, va, vb = [None] * 3, [None] * 3, [None] * 3
    for b in range(3):
        for a in range(3):
            lhs = jnp.concatenate([lwin[2 + a : 42 + a], rwin[1 + a + b : 105 + a + b]], axis=0)
            y = dot(lhs.astype(BF), w[3 * a + b])
            ul[b] = y[:40] if a == 0 else ul[b] + y[:40]
            if a == 0:
                va[b] = y[40:]
            else:
                vb[b] = y[40:] if a == 1 else vb[b] + y[40:]
    u_all[...] = ul[0] + ul[1] + ul[2]
    for var in range(2):
        v = [vb[b] + va[b] if var == 0 else vb[b] for b in range(3)]
        v_all[var] = v[0] + v[1] + v[2]
        e0[var] = ul[1] + ul[2] + (v[1] + v[2])[:40]
        e63[var] = ul[0] + ul[1] + (v[0] + v[1])[63:103]
    tile = lax.broadcasted_iota(jnp.int32, (8, C), 0)

    def row_0(t):
        row = t - 13
        var = jnp.where(first + row == 0, 1, 0)
        pair = (lwin[t + 3 : t + 4] + rwin[t + 3 : t + 67]).astype(BF).astype(F32)
        pre = u_all[t : t + 1] + v_all[var, t : t + BAND]
        pre = jnp.concatenate(
            [
                jnp.where(tile == 0, e0[var, t : t + 1], pre[:8]),
                pre[8 : BAND - 8],
                jnp.where(tile == 7, e63[var, t : t + 1], pre[BAND - 8 :]),
            ],
            axis=0,
        )
        p, sil = gate(0.5 * pre)
        if 12 <= t < 22:
            ds0[t - 12] = slope2(p, sil).astype(BF)
        put(pp1, t, ((pair + sil) * valid(row)).astype(BF), 2, 1)

    copies[1].wait()
    done = 0
    for t0, n in spans(30, 3):
        while done < t0 + n + 4:
            row_0(done)
            done += 1
        x = [pp1[t0 + 2 * a : t0 + 2 * a + n].reshape(n * BAND, 3 * C) for a in range(3)]
        acc = dot(jnp.concatenate(x, axis=1), w[9:18].reshape(9 * C, C))
        for s in range(n):
            t = t0 + s
            p, sil = gate(0.5 * acc[s * BAND : (s + 1) * BAND])
            if 8 <= t < 22:
                ds1[t - 8] = slope2(p, sil).astype(BF)
            pair = pp1[t + 2, :, C : 2 * C].astype(F32)
            put(pp2, t, ((pair + sil) * valid(t - 11)).astype(BF), 4, 1)

    copies[2].wait()

    half = 0.5 * readout

    def top(row, scale):
        return cot_t[:BAND, row + 8 : row + 9] * scale

    for t0, n in spans(22, 4):
        x = [pp2[t0 + 4 * a : t0 + 4 * a + n].reshape(n * BAND, 3 * C) for a in range(3)]
        acc = dot(jnp.concatenate(x, axis=1), w[18:27].reshape(9 * C, C))
        for s in range(n):
            t = t0 + s
            p, sil = gate(0.5 * acc[s * BAND : (s + 1) * BAND])
            if 7 <= t < 15:
                p3[t - 7] = (pp2[t + 4, :, C : 2 * C].astype(F32) + sil).astype(BF)
            put(pd2, t, (top(t - 7, half) * slope2(p, sil)).astype(BF), 4, -1)
    ccv[...] = jnp.zeros((64, HALF), F32)
    rows = [jnp.sum(dot_nt(read_b, p3[s]), axis=0, keepdims=True) for s in range(OWN)]
    ccv[pl.ds(start, OWN), :BAND] = jnp.concatenate(rows, axis=0)

    for t0, n in spans(14, 5):
        x = [pd2[t0 + 8 - 4 * a : t0 + 8 - 4 * a + n].reshape(n * BAND, 3 * C) for a in range(3)]
        acc = dot_nt(jnp.concatenate(x, axis=1), side_by_side(w, 18))
        for s in range(n):
            t = t0 + s
            grad = top(t - 3, readout) + acc[s * BAND : (s + 1) * BAND]
            if 2 <= t < 12:
                g2[t - 2] = grad
            put(pd1, t, (grad * ds1[t].astype(F32) * (0.5 * valid(t - 3))).astype(BF), 2, -1)

    for t0, n in spans(10, 5):
        x = [pd1[t0 + 4 - 2 * a : t0 + 4 - 2 * a + n].reshape(n * BAND, 3 * C) for a in range(3)]
        acc = dot_nt(jnp.concatenate(x, axis=1), side_by_side(w, 9))
        for s in range(n):
            t = t0 + s
            grad = g2[t] + acc[s * BAND : (s + 1) * BAND]
            if 1 <= t < 9:
                hi = grad.astype(BF)
                g1h[t - 1] = hi
                g1l[t - 1] = (grad - hi.astype(F32)).astype(BF)
            d0[t] = (grad * ds0[t].astype(F32) * (0.5 * valid(t - 1))).astype(BF)

    def iotas(shape):
        at = lax.broadcasted_iota(jnp.int32, shape, 1)
        return lax.broadcasted_iota(jnp.int32, shape, 0), at >> 6, at & 63

    def ones(hit):
        return jnp.where(hit, 1.0, 0.0).astype(BF)

    to, i, d = iotas((80, 10 * BAND))
    key = to - i - d
    along = {s: ones(key == s) for s in range(-3, 2)}
    to, i, d = iotas((16, 10 * BAND))
    key = jnp.where(to < OWN, to - i, 99)
    across = [ones(key == a - 2) for a in range(3)]
    unused, i, d = iotas((1, 10 * BAND))
    in_d = [ones((d >= 1 - b) & (d < BAND + 1 - b)) for b in range(3)]
    in_i = [ones((i >= 2 - a) & (i < OWN + 2 - a)) for a in range(3)]
    picks = []
    for a in range(3):
        for b in range(3):
            picks.append(along[a + b - 3] * (in_i[a] * in_d[b]))
            picks.append(across[a] * in_d[b])
    z = dot(jnp.concatenate(picks, axis=0), d0[...].reshape(10 * BAND, C)).astype(BF)
    z = jnp.concatenate([z[96 * k : 96 * k + 96] for k in range(9)], axis=1)
    own = jnp.concatenate([along[-1][:, BAND : 9 * BAND], across[1][:, BAND : 9 * BAND]], axis=0)
    top96 = dot(own, g1h[...].reshape(OWN * BAND, C)) + dot(own, g1l[...].reshape(OWN * BAND, C))
    top96 = top96 + dot_nt(z, side_by_side(w, 0))
    rcv[...] = jnp.zeros((128, C), F32)
    lcv[...] = jnp.zeros((64, C), F32)
    rcv[pl.ds(start, 72)] = top96[:72]
    lcv[pl.ds(start, OWN)] = top96[80:88]
    for j in range(4):
        for g in range(2):
            lanes = slice(HALF * g, HALF * g + HALF)
            out[2 * j + g, 0:16] = rcv[16 * j : 16 * j + 16, lanes]
            out[2 * j + g, 16:32] = rcv[64 + 16 * j : 80 + 16 * j, lanes]
            out[2 * j + g, 32:48] = lcv[16 * j : 16 * j + 16, lanes]
            out[2 * j + g, 48:64] = ccv[16 * j : 16 * j + 16]


def local_part(info, msg, w_own, w_z, w_s):
    vm = pltpu.VMEM
    scratch = [
        vm((27, C, C), BF),
        vm((176, C), F32),
        vm((176, C), F32),
        vm((192, HALF), F32),
        vm((48, C), F32),
        vm((112, C), F32),
        vm((40, C), F32),
        vm((2, 104, C), F32),
        vm((2, 40, C), F32),
        vm((2, 40, C), F32),
        vm((34, BAND, 3 * C), BF),
        vm((30, BAND, 3 * C), BF),
        vm((22, BAND, 3 * C), BF),
        vm((14, BAND, 3 * C), BF),
        vm((10, BAND, C), BF),
        vm((14, BAND, C), BF),
        vm((10, BAND, C), F32),
        vm((8, BAND, C), BF),
        vm((10, BAND, C), BF),
        vm((8, BAND, C), BF),
        vm((8, BAND, C), BF),
        vm((128, C), F32),
        vm((64, C), F32),
        vm((64, HALF), F32),
        pltpu.SemaphoreType.DMA((5,)),
    ]
    return pl.pallas_call(
        body,
        out_shape=jax.ShapeDtypeStruct((8, 64, HALF), F32),
        in_specs=[
            pl.BlockSpec(memory_space=pltpu.SMEM),
            pl.BlockSpec(memory_space=vm),
            pl.BlockSpec(memory_space=pl.ANY),
            pl.BlockSpec(memory_space=pl.ANY),
            pl.BlockSpec(memory_space=pl.ANY),
        ],
        out_specs=pl.BlockSpec(memory_space=vm),
        scratch_shapes=scratch,
        compiler_params=pltpu.CompilerParams(vmem_limit_bytes=48 * 2**20),
        cost_estimate=pl.CostEstimate(
            flops=6 * 10**9, bytes_accessed=5 * 10**6, transcendentals=2 * 10**6
        ),
        name="decoder",
    )(info, msg, w_own, w_z, w_s)


def z_pairs(chroms):
    pairs = []
    per_z = chroms // 4
    for ch in range(chroms):
        hi, rest = ch // per_z, ch % per_z
        for g in range(2):
            step = (1 if g == 0 else -1) * (1 if ch % 2 == 0 else -1)
            z = (2 * hi + g + step) % 8
            pairs.append((((z // 2) * per_z + rest) * 2 + z % 2, 2 * ch + g))
    return pairs


def parts_of(x, count):
    parts = []
    for _ in range(count):
        hi = lax.reduce_precision(x, 8, 7)
        parts.append(hi.astype(BF))
        x = x - hi
    return parts


def local(left, right, weight, readout, cotangent):
    rows = left.shape[0]
    chroms = lax.axis_size(CHROM)
    slab = lax.axis_index(CHROM)
    core = lax.axis_index("core")
    chan = lax.axis_index("chan")
    own_w = weight.reshape(27, C, HALF)
    piece = jnp.where(core == 0, own_w[:14], own_w[13:])

    hi, lo = parts_of(cotangent, 2)
    read = jnp.pad(jnp.stack(parts_of(readout, 3)).reshape(6, BAND), ((0, rows - 6), (0, 0)))
    cot = jnp.concatenate([jnp.where(chan == 0, hi, lo), read], axis=1)
    mine = jnp.concatenate([left, right, cot], axis=0)
    piece, mine = lax.optimization_barrier((piece, mine))
    w_z = lax.ppermute(piece, "chan", [(0, 1), (1, 0)])
    slabs = 4
    groups = chroms // slabs
    next_group = [
        (slabs * (g + 1) + j, slabs * g + j) for g in range(groups - 1) for j in range(slabs)
    ]
    ends = [(slabs * g + 3, slabs * (g + 1) + 1) for g in range(groups - 1)]
    ends += [(slabs * (g + 2), slabs * g + 3) for g in range(groups - 2)]
    after = lax.ppermute(mine, CHROM, next_group)
    edge = lax.ppermute(mine, CHROM, ends)
    extra = jnp.where(slab % slabs == 0, after, edge)
    block = jnp.concatenate([mine, after[rows : 2 * rows], extra], axis=0)
    msg = lax.all_to_all(
        jnp.broadcast_to(block[None], (8,) + block.shape), GROUP, 0, 0, tiled=False
    )
    msg, w_z = lax.optimization_barrier((msg, w_z))
    w_s = lax.ppermute(w_z, "core", [(0, 1), (1, 0)])
    q = lax.axis_index(GROUP)
    info = jnp.stack(
        [q, rows * slab + OWN * chan, core, chan, rows * chroms]
    ).astype(jnp.int32)
    sent = local_part(info, msg, own_w, w_z, w_s)
    got = jnp.sum(lax.all_to_all(sent, GROUP, 0, 0, tiled=False), axis=0)
    moved = lax.ppermute(got[16:32], CHROM, [(b, a) for a, b in next_group])
    return got[48:64, :BAND], got[32:48], got[0:16] + moved


def solution(mesh):
    chroms = mesh.shape["chrom"]
    small = Mesh(
        mesh.devices.reshape(chroms // 16, 4, 2, 2, 2), ("h", "yh", "yl", "core", "chan")
    )
    return jax.shard_map(
        local,
        mesh=small,
        in_specs=(
            P(CHROM, "chan"),
            P(CHROM, "chan"),
            P(None, None, None, None, "chan"),
            P("chan"),
            P(CHROM, None),
        ),
        out_specs=(P(CHROM, None), P(CHROM, "chan"), P(CHROM, "chan")),
        check_vma=False,
    )
```

time: 88.7 us -> 70.5 us (0.79)
  the two profiles are of different devices: /device:TPU:128 before, /device:TPU:256 now
where the time goes in v2:
time: 70.5 us; the launch traced here: 70.1 us
  blocking collectives  21.2 us (30%)
  starting transfers between devices  20.3 us (29%)
  waiting for transfers between devices  11.3 us (16%)
  Pallas kernels  10.9 us (15%)
  other arithmetic  4.72 us (7%)
  local copies, waits for them, and re-layouts  0.82 us (1%)
  between operations  0.79 us (1%)
    all_to_all x1, blocking collectives, local(): lax.all_to_all(jnp.broadcast_to(block[None], (8,) + block.shape), GROUP,...  12.7 us
    pallas_call x1, Pallas kernels, local_part(): pl.pallas_call(body, out_shape=jax.ShapeDtypeStruct((8, 64, HALF), F32),...  10.9 us
    all_to_all x1, blocking collectives, local(): got = jnp.sum(lax.all_to_all(sent, GROUP, 0, 0, tiled=False), axis=0)  8.52 us
    ppermute x1, waiting for transfers between devices, local(): moved = lax.ppermute(got[16:32], CHROM, [(b, a) for a, b in next_group])  7.85 us
    ppermute x1, starting transfers between devices, local(): after = lax.ppermute(mine, CHROM, next_group)  7.44 us
    ppermute x1, starting transfers between devices, local(): moved = lax.ppermute(got[16:32], CHROM, [(b, a) for a, b in next_group])  4.41 us
    ppermute x1, starting transfers between devices, local(): w_z = lax.ppermute(piece, 'chan', [(0, 1), (1, 0)])  3.37 us
    ppermute x1, starting transfers between devices, local(): edge = lax.ppermute(mine, CHROM, ends)  2.8 us
  transfers between devices with their start and end apart: 5, of which 3 were waited for; matrix products, arithmetic and copies ran while one was open for 1% of the time, Pallas kernels for 0%

profile of v2, /device:TPU:256, one launch (start us, length us, event | category | flops | bytes accessed | tf_op | source)
XLA Modules:
  0.0 70.1 jit_solution(16447577330865329554)
XLA Ops:
  0.6 0.0 copy-start.1
  0.6 0.0 copy-start.2
  0.7 0.7 fusion.8
  1.3 0.1 reshape.14
  1.4 0.7 %fusion.7 = bf16[16,64]{1,0:T(8,128)(2,1)S(1)} fusion(f32[16,64]{1,0:T(8,128)} %param.9, pred[]{:T(512)S(6)} %eq.12), kind=kLoop, calls=%fused_computation.15 | loop fusion | flops 6144 | bytes 6145 | tf_op jit(solution)/shard_map/jit(_where)/select_n | solution.py:339
  2.1 0.0 copy-start
  2.1 2.6 %slice_select_fusion = bf16[14,256,128]{2,1,0:T(8,128)(2,1)} fusion(bf16[27,256,128]{2,1,0:T(8,128)(2,1)} %bitcast.11, pred[]{:T(512)S(6)} %eq.11), kind=kLoop, calls=%fused_computation | loop fusion | flops 458752 | bytes 2752513 | tf_op jit(solution)/shard_map/jit(_where)/select_n | solution.py:335
  4.8 0.0 copy-done.1
  4.8 0.0 copy-done.2
  4.8 0.1 fusion.4
  4.8 3.4 %collective-permute-start.2 = (bf16[14,256,128]{2,1,0:T(8,128)(2,1)}, bf16[14,256,128]{2,1,0:T(8,128)(2,1)S(1)}, u32[]{:S(2)}, u32[]{:S(2)}) collective-permute-start(bf16[14,256,128]{2,1,0:T(8,128)(2,1)} %slice_select_fusion), channel_id=1, source_target_pairs={{0,1},{1,0},{2,3},{3,2},{4,5},{5,4},{6,7},{7,6},{8,9},{9,8},{10,11... | collective-permute-start | bytes 2752520 | tf_op jit(solution)/shard_map/ppermute | solution.py:342
  8.2 7.4 %collective-permute-start = (bf16[48,128]{1,0:T(8,128)(2,1)S(1)}, bf16[48,128]{1,0:T(8,128)(2,1)S(1)}, u32[]{:S(2)}, u32[]{:S(2)}) collective-permute-start(bf16[48,128]{1,0:T(8,128)(2,1)S(1)} %fusion.4), channel_id=1, source_target_pairs={{8,0},{10,2},{12,4},{14,6},{16,8},{18,10},{20,12},{22,14},{24,16},... | collective-permute-start | bytes 36872 | tf_op jit(solution)/shard_map/ppermute | solution.py:350
  15.7 2.8 %collective-permute-start.1 = (bf16[48,128]{1,0:T(8,128)(2,1)S(1)}, bf16[48,128]{1,0:T(8,128)(2,1)S(1)}, u32[]{:S(2)}, u32[]{:S(2)}) collective-permute-start(bf16[48,128]{1,0:T(8,128)(2,1)S(1)} %fusion.4), channel_id=1, source_target_pairs={{6,10},{14,18},{22,26},{30,34},{38,42},{46,50},{54,58},{62,66},{70... | collective-permute-start | bytes 36872 | tf_op jit(solution)/shard_map/ppermute | solution.py:351
  18.5 0.0 collective-permute-done
  18.5 1.3 %collective-permute-done.1 = bf16[48,128]{1,0:T(8,128)(2,1)S(1)} collective-permute-done((bf16[48,128]{1,0:T(8,128)(2,1)S(1)}, bf16[48,128]{1,0:T(8,128)(2,1)S(1)}, u32[]{:S(2)}, u32[]{:S(2)}) %collective-permute-start.1) | collective-permute-done | bytes 12320 | tf_op jit(solution)/shard_map/ppermute | solution.py:351
  19.9 12.7 %all_to_all.10.msg = bf16[8,112,128]{2,1,0:T(8,128)(2,1)S(1)} all-to-all(bf16[8,112,128]{2,1,0:T(8,128)(2,1)S(1)} %broadcast_in_dim.2), channel_id=1, replica_groups=mesh['h'=16,'yh'=4,'yl'=2,'core'=2,'chan'=2] {'yl','core','chan'}, dimensions={0} | all-to-all | bytes 458752 | tf_op jit(solution)/shard_map/all_to_all | solution.py:354
  32.6 0.0 collective-permute-done.2.w_z
  32.6 2.3 %collective-permute-start.3 = (bf16[14,256,128]{2,1,0:T(8,128)(2,1)S(1)}, bf16[14,256,128]{2,1,0:T(8,128)(2,1)}, u32[]{:S(2)}, u32[]{:S(2)}) collective-permute-start(bf16[14,256,128]{2,1,0:T(8,128)(2,1)S(1)} %collective-permute-done.2.w_z), channel_id=1, source_target_pairs={{0,2},{2,0},{1,3},{3,1},{4,6},{6,4},{5,7},{7,5},{8,10},{10,8},{9,1... | collective-permute-start | bytes 2752520 | tf_op jit(solution)/shard_map/ppermute | solution.py:358
  35.0 0.1 stack.31.info
  35.0 2.1 %collective-permute-done.3.w_s = bf16[14,256,128]{2,1,0:T(8,128)(2,1)} collective-permute-done((bf16[14,256,128]{2,1,0:T(8,128)(2,1)S(1)}, bf16[14,256,128]{2,1,0:T(8,128)(2,1)}, u32[]{:S(2)}, u32[]{:S(2)}) %collective-permute-start.3) | collective-permute-done | bytes 917536 | tf_op jit(solution)/shard_map/ppermute | solution.py:358
  37.2 0.0 copy-done
  37.2 10.9 %decoder.1 = f32[8,64,128]{2,1,0:T(8,128)S(1)} custom-call(s32[5]{0:T(128)S(1)} %stack.31.info, bf16[8,112,128]{2,1,0:T(8,128)(2,1)S(1)} %all_to_all.10.msg, bf16[27,256,128]{2,1,0:T(8,128)(2,1)S(1)} %bitcast.12, bf16[14,256,128]{2,1,0:T(8,128)(2,1)S(1)} %collective-permute-done.2.w_z, bf16[14,256,128]{2,1,0:T(8,128)(2,1)} %collective-permute-done.3.w_s), custom_call_target="tpu_custom_call" | custom-call | flops 6000000000 | bytes 5000000 | tf_op jit(solution)/shard_map/decoder/pallas_call | solution.py:287
  48.1 8.5 %all_to_all.11 = f32[8,64,128]{2,1,0:T(8,128)S(1)} all-to-all(f32[8,64,128]{2,1,0:T(8,128)S(1)} %decoder.1), channel_id=1, replica_groups=mesh['h'=16,'yh'=4,'yl'=2,'core'=2,'chan'=2] {'yl','core','chan'}, dimensions={0} | all-to-all | bytes 524288 | tf_op jit(solution)/shard_map/all_to_all | solution.py:364
  56.7 4.4 %collective-permute-start.4 = (f32[16,128]{1,0:T(8,128)S(1)}, f32[16,128]{1,0:T(8,128)S(1)}, u32[]{:S(2)}, u32[]{:S(2)}) collective-permute-start(f32[16,128]{1,0:T(8,128)S(1)} %slice.34), channel_id=1, source_target_pairs={{0,8},{2,10},{4,12},{6,14},{8,16},{10,18},{12,20},{14,22},{16,24},... | collective-permute-start | bytes 24584 | tf_op jit(solution)/shard_map/ppermute | solution.py:365
  61.1 0.6 slice.31
  61.7 7.8 %collective-permute-done.4 = f32[16,128]{1,0:T(8,128)S(1)} collective-permute-done((f32[16,128]{1,0:T(8,128)S(1)}, f32[16,128]{1,0:T(8,128)S(1)}, u32[]{:S(2)}, u32[]{:S(2)}) %collective-permute-start.4) | collective-permute-done | bytes 8224 | tf_op jit(solution)/shard_map/ppermute | solution.py:365
  69.5 0.6 slice_add_fusion
  (7 shorter events, 0.1 us)
Async XLA Ops:
  0.6 4.1 %copy-start.1 = (bf16[16,128]{1,0:T(8,128)(2,1)S(1)}, bf16[16,128]{1,0:T(8,128)(2,1)}, u32[]{:S(2)}) copy-start(bf16[16,128]{1,0:T(8,128)(2,1)} %param.6) | copy-start | bytes 12292
  0.6 4.1 %copy-start.2 = (bf16[16,128]{1,0:T(8,128)(2,1)S(1)}, bf16[16,128]{1,0:T(8,128)(2,1)}, u32[]{:S(2)}) copy-start(bf16[16,128]{1,0:T(8,128)(2,1)} %param.5) | copy-start | bytes 12292
  2.1 35.0 %copy-start = (bf16[3,3,3,256,128]{4,3,2,1,0:T(8,128)(2,1)S(1)}, bf16[3,3,3,256,128]{4,3,2,1,0:T(8,128)(2,1)}, u32[]{:S(2)}) copy-start(bf16[3,3,3,256,128]{4,3,2,1,0:T(8,128)(2,1)} %param.7) | copy-start | bytes 5308420
  4.8 27.8 %collective-permute-start.2 = (bf16[14,256,128]{2,1,0:T(8,128)(2,1)}, bf16[14,256,128]{2,1,0:T(8,128)(2,1)S(1)}, u32[]{:S(2)}, u32[]{:S(2)}) collective-permute-start(bf16[14,256,128]{2,1,0:T(8,128)(2,1)} %slice_select_fusion), channel_id=1, source_target_pairs={{0,1},{1,0},{2,3},{3,2},{4,5},{5,4},{6,7},{7,6},{8,9},{9,8},{10,11... | collective-permute-start | bytes 2752520 | tf_op jit(solution)/shard_map/ppermute | solution.py:342
  8.2 10.3 %collective-permute-start = (bf16[48,128]{1,0:T(8,128)(2,1)S(1)}, bf16[48,128]{1,0:T(8,128)(2,1)S(1)}, u32[]{:S(2)}, u32[]{:S(2)}) collective-permute-start(bf16[48,128]{1,0:T(8,128)(2,1)S(1)} %fusion.4), channel_id=1, source_target_pairs={{8,0},{10,2},{12,4},{14,6},{16,8},{18,10},{20,12},{22,14},{24,16},... | collective-permute-start | bytes 36872 | tf_op jit(solution)/shard_map/ppermute | solution.py:350
  15.7 4.2 %collective-permute-start.1 = (bf16[48,128]{1,0:T(8,128)(2,1)S(1)}, bf16[48,128]{1,0:T(8,128)(2,1)S(1)}, u32[]{:S(2)}, u32[]{:S(2)}) collective-permute-start(bf16[48,128]{1,0:T(8,128)(2,1)S(1)} %fusion.4), channel_id=1, source_target_pairs={{6,10},{14,18},{22,26},{30,34},{38,42},{46,50},{54,58},{62,66},{70... | collective-permute-start | bytes 36872 | tf_op jit(solution)/shard_map/ppermute | solution.py:351
  32.6 4.5 %collective-permute-start.3 = (bf16[14,256,128]{2,1,0:T(8,128)(2,1)S(1)}, bf16[14,256,128]{2,1,0:T(8,128)(2,1)}, u32[]{:S(2)}, u32[]{:S(2)}) collective-permute-start(bf16[14,256,128]{2,1,0:T(8,128)(2,1)S(1)} %collective-permute-done.2.w_z), channel_id=1, source_target_pairs={{0,2},{2,0},{1,3},{3,1},{4,6},{6,4},{5,7},{7,5},{8,10},{10,8},{9,1... | collective-permute-start | bytes 2752520 | tf_op jit(solution)/shard_map/ppermute | solution.py:358
  56.7 12.9 %collective-permute-start.4 = (f32[16,128]{1,0:T(8,128)S(1)}, f32[16,128]{1,0:T(8,128)S(1)}, u32[]{:S(2)}, u32[]{:S(2)}) collective-permute-start(f32[16,128]{1,0:T(8,128)S(1)} %slice.34), channel_id=1, source_target_pairs={{0,8},{2,10},{4,12},{6,14},{8,16},{10,18},{12,20},{14,22},{16,24},... | collective-permute-start | bytes 24584 | tf_op jit(solution)/shard_map/ppermute | solution.py:365

commit v3 on v2

--- a/solution.py
+++ b/solution.py
@@ -192,7 +192,9 @@
             put(pd2, t, (top(t - 7, half) * slope2(p, sil)).astype(BF), 4, -1)
     ccv[...] = jnp.zeros((64, HALF), F32)
     rows = [jnp.sum(dot_nt(read_b, p3[s]), axis=0, keepdims=True) for s in range(OWN)]
-    ccv[pl.ds(start, OWN), :BAND] = jnp.concatenate(rows, axis=0)
+    contact = jnp.concatenate(rows, axis=0)
+    hi = contact.astype(BF).astype(F32)
+    ccv[pl.ds(start, OWN)] = jnp.concatenate([hi, contact - hi], axis=1)
 
     for t0, n in spans(14, 5):
         x = [pd2[t0 + 8 - 4 * a : t0 + 8 - 4 * a + n].reshape(n * BAND, 3 * C) for a in range(3)]
@@ -249,10 +251,10 @@
     for j in range(4):
         for g in range(2):
             lanes = slice(HALF * g, HALF * g + HALF)
-            out[2 * j + g, 0:16] = rcv[16 * j : 16 * j + 16, lanes]
-            out[2 * j + g, 16:32] = rcv[64 + 16 * j : 80 + 16 * j, lanes]
-            out[2 * j + g, 32:48] = lcv[16 * j : 16 * j + 16, lanes]
-            out[2 * j + g, 48:64] = ccv[16 * j : 16 * j + 16]
+            out[2 * j + g, 0:16] = rcv[16 * j : 16 * j + 16, lanes].astype(BF)
+            out[2 * j + g, 16:32] = rcv[64 + 16 * j : 80 + 16 * j, lanes].astype(BF)
+            out[2 * j + g, 32:48] = lcv[16 * j : 16 * j + 16, lanes].astype(BF)
+            out[2 * j + g, 48:64] = ccv[16 * j : 16 * j + 16].astype(BF)
 
 
 def local_part(info, msg, w_own, w_z, w_s):
@@ -286,7 +288,7 @@
     ]
     return pl.pallas_call(
         body,
-        out_shape=jax.ShapeDtypeStruct((8, 64, HALF), F32),
+        out_shape=jax.ShapeDtypeStruct((8, 64, HALF), BF),
         in_specs=[
             pl.BlockSpec(memory_space=pltpu.SMEM),
             pl.BlockSpec(memory_space=vm),
@@ -316,6 +318,31 @@
     return pairs
 
 
+def copy_taps(core, w_own, out, sem):
+    moves = [
+        pltpu.make_async_copy(
+            w_own.at[pl.ds(core[0] * 13 + 2 * k, 2)], out.at[pl.ds(2 * k, 2)], sem.at[k]
+        )
+        for k in range(7)
+    ]
+    for move in moves:
+        move.start()
+    for move in moves:
+        move.wait()
+
+
+def own_taps(core, w_own):
+    return pl.pallas_call(
+        copy_taps,
+        out_shape=jax.ShapeDtypeStruct((14, C, HALF), BF),
+        in_specs=[pl.BlockSpec(memory_space=pltpu.SMEM), pl.BlockSpec(memory_space=pl.ANY)],
+        out_specs=pl.BlockSpec(memory_space=pltpu.VMEM),
+        scratch_shapes=[pltpu.SemaphoreType.DMA((7,))],
+        cost_estimate=pl.CostEstimate(flops=0, bytes_accessed=2 * 10**6, transcendentals=0),
+        name="own_taps",
+    )(core, w_own)
+
+
 def parts_of(x, count):
     parts = []
     for _ in range(count):
@@ -332,7 +359,8 @@
     core = lax.axis_index("core")
     chan = lax.axis_index("chan")
     own_w = weight.reshape(27, C, HALF)
-    piece = jnp.where(core == 0, own_w[:14], own_w[13:])
+    piece = own_taps(core[None].astype(jnp.int32), own_w)
+    piece, readout, cotangent = lax.optimization_barrier((piece, readout, cotangent))
 
     hi, lo = parts_of(cotangent, 2)
     read = jnp.pad(jnp.stack(parts_of(readout, 3)).reshape(6, BAND), ((0, rows - 6), (0, 0)))
@@ -361,9 +389,9 @@
         [q, rows * slab + OWN * chan, core, chan, rows * chroms]
     ).astype(jnp.int32)
     sent = local_part(info, msg, own_w, w_z, w_s)
-    got = jnp.sum(lax.all_to_all(sent, GROUP, 0, 0, tiled=False), axis=0)
+    got = jnp.sum(lax.all_to_all(sent, GROUP, 0, 0, tiled=False).astype(F32), axis=0)
     moved = lax.ppermute(got[16:32], CHROM, [(b, a) for a, b in next_group])
-    return got[48:64, :BAND], got[32:48], got[0:16] + moved
+    return got[48:64, :BAND] + got[48:64, BAND:], got[32:48], got[0:16] + moved
 
 
 def solution(mesh):

time: 70.5 us -> 67.8 us (0.962)
  other arithmetic: 4.72 us -> 1.42 us
  Pallas kernels: 10.9 us -> 13.3 us
  blocking collectives: 21.2 us -> 20.2 us
    select_n x1 -> x0, other arithmetic: 2.63 us -> none  [local(): piece = jnp.where(core == 0, own_w[:14], own_w[13:])]
    pallas_call x1 -> x2, Pallas kernels: 10.9 us -> 13.3 us  [the longest x1 10.9 us: local_part(): pl.pallas_call(body, out_shape=jax.ShapeDtypeStruct((8, 64, HALF), BF), i...]
    all_to_all x1, blocking collectives: 8.52 us -> 7.45 us  [local(): lax.all_to_all(sent, GROUP, 0, 0, tiled=False).astype(F32)]
where the time goes in v3:
time: 67.8 us; the launch traced here: 67.4 us
  starting transfers between devices  20.3 us (30%)
  blocking collectives  20.2 us (30%)
  Pallas kernels  13.3 us (20%)
  waiting for transfers between devices  11.2 us (17%)
  other arithmetic  1.42 us (2%)
  between operations  0.85 us (1%)
    all_to_all x1, blocking collectives, local(): lax.all_to_all(jnp.broadcast_to(block[None], (8,) + block.shape), GROUP,...  12.7 us
    pallas_call x1, Pallas kernels, local_part(): pl.pallas_call(body, out_shape=jax.ShapeDtypeStruct((8, 64, HALF), BF), i...  10.9 us
    ppermute x1, waiting for transfers between devices, local(): moved = lax.ppermute(got[16:32], CHROM, [(b, a) for a, b in next_group])  7.71 us
    all_to_all x1, blocking collectives, local(): lax.all_to_all(sent, GROUP, 0, 0, tiled=False).astype(F32)  7.45 us
    ppermute x1, starting transfers between devices, local(): after = lax.ppermute(mine, CHROM, next_group)  7.44 us
    ppermute x1, starting transfers between devices, local(): moved = lax.ppermute(got[16:32], CHROM, [(b, a) for a, b in next_group])  4.38 us
    ppermute x1, starting transfers between devices, local(): w_z = lax.ppermute(piece, 'chan', [(0, 1), (1, 0)])  3.37 us
    ppermute x1, starting transfers between devices, local(): edge = lax.ppermute(mine, CHROM, ends)  2.8 us
  transfers between devices with their start and end apart: 5, of which 3 were waited for; matrix products, arithmetic and copies ran while one was open for 1% of the time, Pallas kernels for 0%

profile of v3, /device:TPU:256, one launch (start us, length us, event | category | flops | bytes accessed | tf_op | source)
XLA Modules:
  0.0 67.4 jit_solution(12007003745614200047)
XLA Ops:
  0.6 0.0 copy-start.1
  0.6 0.0 copy-start.4
  0.7 0.0 copy-start.2
  0.7 0.0 copy-start.3
  0.7 0.0 copy-start
  0.7 2.4 %own_taps.1 = bf16[14,256,128]{2,1,0:T(8,128)(2,1)} custom-call(s32[1]{0:T(128)} %bitcast.2.core, bf16[27,256,128]{2,1,0:T(8,128)(2,1)} %bitcast.11), custom_call_target="tpu_custom_call" | custom-call | bytes 2000000 | tf_op jit(solution)/shard_map/own_taps/pallas_call | solution.py:335
  3.1 0.0 copy-done.4
  3.1 0.1 reshape.14
  3.2 0.0 copy-done.1
  3.2 0.0 copy-done.2
  3.2 0.0 copy-done.3
  3.2 0.1 fusion.4
  3.3 3.4 %collective-permute-start.2 = (bf16[14,256,128]{2,1,0:T(8,128)(2,1)}, bf16[14,256,128]{2,1,0:T(8,128)(2,1)S(1)}, u32[]{:S(2)}, u32[]{:S(2)}) collective-permute-start(bf16[14,256,128]{2,1,0:T(8,128)(2,1)} %own_taps.1), channel_id=1, source_target_pairs={{0,1},{1,0},{2,3},{3,2},{4,5},{5,4},{6,7},{7,6},{8,9},{9,8},{10,11... | collective-permute-start | bytes 2752520 | tf_op jit(solution)/shard_map/ppermute | solution.py:370
  6.7 7.4 %collective-permute-start = (bf16[48,128]{1,0:T(8,128)(2,1)S(1)}, bf16[48,128]{1,0:T(8,128)(2,1)S(1)}, u32[]{:S(2)}, u32[]{:S(2)}) collective-permute-start(bf16[48,128]{1,0:T(8,128)(2,1)S(1)} %fusion.4), channel_id=1, source_target_pairs={{8,0},{10,2},{12,4},{14,6},{16,8},{18,10},{20,12},{22,14},{24,16},... | collective-permute-start | bytes 36872 | tf_op jit(solution)/shard_map/ppermute | solution.py:378
  14.1 2.8 %collective-permute-start.1 = (bf16[48,128]{1,0:T(8,128)(2,1)S(1)}, bf16[48,128]{1,0:T(8,128)(2,1)S(1)}, u32[]{:S(2)}, u32[]{:S(2)}) collective-permute-start(bf16[48,128]{1,0:T(8,128)(2,1)S(1)} %fusion.4), channel_id=1, source_target_pairs={{6,10},{14,18},{22,26},{30,34},{38,42},{46,50},{54,58},{62,66},{70... | collective-permute-start | bytes 36872 | tf_op jit(solution)/shard_map/ppermute | solution.py:379
  16.9 0.0 collective-permute-done
  17.0 1.3 %collective-permute-done.1 = bf16[48,128]{1,0:T(8,128)(2,1)S(1)} collective-permute-done((bf16[48,128]{1,0:T(8,128)(2,1)S(1)}, bf16[48,128]{1,0:T(8,128)(2,1)S(1)}, u32[]{:S(2)}, u32[]{:S(2)}) %collective-permute-start.1) | collective-permute-done | bytes 12320 | tf_op jit(solution)/shard_map/ppermute | solution.py:379
  18.4 12.7 %all_to_all.10.msg = bf16[8,112,128]{2,1,0:T(8,128)(2,1)S(1)} all-to-all(bf16[8,112,128]{2,1,0:T(8,128)(2,1)S(1)} %broadcast_in_dim.2), channel_id=1, replica_groups=mesh['h'=16,'yh'=4,'yl'=2,'core'=2,'chan'=2] {'yl','core','chan'}, dimensions={0} | all-to-all | bytes 458752 | tf_op jit(solution)/shard_map/all_to_all | solution.py:382
  31.1 0.0 collective-permute-done.2.w_z
  31.1 2.3 %collective-permute-start.3 = (bf16[14,256,128]{2,1,0:T(8,128)(2,1)S(1)}, bf16[14,256,128]{2,1,0:T(8,128)(2,1)}, u32[]{:S(2)}, u32[]{:S(2)}) collective-permute-start(bf16[14,256,128]{2,1,0:T(8,128)(2,1)S(1)} %collective-permute-done.2.w_z), channel_id=1, source_target_pairs={{0,2},{2,0},{1,3},{3,1},{4,6},{6,4},{5,7},{7,5},{8,10},{10,8},{9,1... | collective-permute-start | bytes 2752520 | tf_op jit(solution)/shard_map/ppermute | solution.py:386
  33.4 0.1 stack.31.info
  33.5 2.1 %collective-permute-done.3.w_s = bf16[14,256,128]{2,1,0:T(8,128)(2,1)} collective-permute-done((bf16[14,256,128]{2,1,0:T(8,128)(2,1)S(1)}, bf16[14,256,128]{2,1,0:T(8,128)(2,1)}, u32[]{:S(2)}, u32[]{:S(2)}) %collective-permute-start.3) | collective-permute-done | bytes 917536 | tf_op jit(solution)/shard_map/ppermute | solution.py:386
  35.6 0.0 copy-done
  35.6 10.9 %decoder.1 = bf16[8,64,128]{2,1,0:T(8,128)(2,1)S(1)} custom-call(s32[5]{0:T(128)S(1)} %stack.31.info, bf16[8,112,128]{2,1,0:T(8,128)(2,1)S(1)} %all_to_all.10.msg, bf16[27,256,128]{2,1,0:T(8,128)(2,1)S(1)} %bitcast.12, bf16[14,256,128]{2,1,0:T(8,128)(2,1)S(1)} %collective-permute-done.2.w_z, bf16[14,256,128]{2,1,0:T(8,128)(2,1)} %collective-permute-done.3.w_s), custom_call_target="tpu_custom_call" | custom-call | flops 6000000000 | bytes 5000000 | tf_op jit(solution)/shard_map/decoder/pallas_call | solution.py:289
  46.5 7.4 %all_to_all.11 = bf16[8,64,128]{2,1,0:T(8,128)(2,1)S(1)} all-to-all(bf16[8,64,128]{2,1,0:T(8,128)(2,1)S(1)} %decoder.1), channel_id=1, replica_groups=mesh['h'=16,'yh'=4,'yl'=2,'core'=2,'chan'=2] {'yl','core','chan'}, dimensions={0} | all-to-all | bytes 262144 | tf_op jit(solution)/shard_map/all_to_all | solution.py:392
  54.0 4.4 %collective-permute-start.4 = (f32[16,128]{1,0:T(8,128)S(1)}, f32[16,128]{1,0:T(8,128)S(1)}, u32[]{:S(2)}, u32[]{:S(2)}) collective-permute-start(f32[16,128]{1,0:T(8,128)S(1)} %slice.29), channel_id=1, source_target_pairs={{0,8},{2,10},{4,12},{6,14},{8,16},{10,18},{12,20},{14,22},{16,24},... | collective-permute-start | bytes 24584 | tf_op jit(solution)/shard_map/ppermute | solution.py:393
  58.4 0.7 slice_add_fusion.1
  59.1 7.7 %collective-permute-done.4 = f32[16,128]{1,0:T(8,128)S(1)} collective-permute-done((f32[16,128]{1,0:T(8,128)S(1)}, f32[16,128]{1,0:T(8,128)S(1)}, u32[]{:S(2)}, u32[]{:S(2)}) %collective-permute-start.4) | collective-permute-done | bytes 8224 | tf_op jit(solution)/shard_map/ppermute | solution.py:393
  66.8 0.6 slice_add_fusion
  (9 shorter events, 0.1 us)
Async XLA Ops:
  0.6 2.6 %copy-start.1 = (f32[16,64]{1,0:T(8,128)S(1)}, f32[16,64]{1,0:T(8,128)}, u32[]{:S(2)}) copy-start(f32[16,64]{1,0:T(8,128)} %param.9) | copy-start | bytes 12292
  0.6 2.4 %copy-start.4 = (f32[128]{0:T(128)S(1)}, f32[128]{0:T(128)}, u32[]{:S(2)}) copy-start(f32[128]{0:T(128)} %param.8) | copy-start | bytes 1540
  0.7 2.5 %copy-start.2 = (bf16[16,128]{1,0:T(8,128)(2,1)S(1)}, bf16[16,128]{1,0:T(8,128)(2,1)}, u32[]{:S(2)}) copy-start(bf16[16,128]{1,0:T(8,128)(2,1)} %param.6) | copy-start | bytes 12292
  0.7 2.5 %copy-start.3 = (bf16[16,128]{1,0:T(8,128)(2,1)S(1)}, bf16[16,128]{1,0:T(8,128)(2,1)}, u32[]{:S(2)}) copy-start(bf16[16,128]{1,0:T(8,128)(2,1)} %param.5) | copy-start | bytes 12292
  0.7 34.9 %copy-start = (bf16[3,3,3,256,128]{4,3,2,1,0:T(8,128)(2,1)S(1)}, bf16[3,3,3,256,128]{4,3,2,1,0:T(8,128)(2,1)}, u32[]{:S(2)}) copy-start(bf16[3,3,3,256,128]{4,3,2,1,0:T(8,128)(2,1)} %param.7) | copy-start | bytes 5308420
  3.3 27.8 %collective-permute-start.2 = (bf16[14,256,128]{2,1,0:T(8,128)(2,1)}, bf16[14,256,128]{2,1,0:T(8,128)(2,1)S(1)}, u32[]{:S(2)}, u32[]{:S(2)}) collective-permute-start(bf16[14,256,128]{2,1,0:T(8,128)(2,1)} %own_taps.1), channel_id=1, source_target_pairs={{0,1},{1,0},{2,3},{3,2},{4,5},{5,4},{6,7},{7,6},{8,9},{9,8},{10,11... | collective-permute-start | bytes 2752520 | tf_op jit(solution)/shard_map/ppermute | solution.py:370
  6.7 10.3 %collective-permute-start = (bf16[48,128]{1,0:T(8,128)(2,1)S(1)}, bf16[48,128]{1,0:T(8,128)(2,1)S(1)}, u32[]{:S(2)}, u32[]{:S(2)}) collective-permute-start(bf16[48,128]{1,0:T(8,128)(2,1)S(1)} %fusion.4), channel_id=1, source_target_pairs={{8,0},{10,2},{12,4},{14,6},{16,8},{18,10},{20,12},{22,14},{24,16},... | collective-permute-start | bytes 36872 | tf_op jit(solution)/shard_map/ppermute | solution.py:378
  14.1 4.2 %collective-permute-start.1 = (bf16[48,128]{1,0:T(8,128)(2,1)S(1)}, bf16[48,128]{1,0:T(8,128)(2,1)S(1)}, u32[]{:S(2)}, u32[]{:S(2)}) collective-permute-start(bf16[48,128]{1,0:T(8,128)(2,1)S(1)} %fusion.4), channel_id=1, source_target_pairs={{6,10},{14,18},{22,26},{30,34},{38,42},{46,50},{54,58},{62,66},{70... | collective-permute-start | bytes 36872 | tf_op jit(solution)/shard_map/ppermute | solution.py:379
  31.1 4.5 %collective-permute-start.3 = (bf16[14,256,128]{2,1,0:T(8,128)(2,1)S(1)}, bf16[14,256,128]{2,1,0:T(8,128)(2,1)}, u32[]{:S(2)}, u32[]{:S(2)}) collective-permute-start(bf16[14,256,128]{2,1,0:T(8,128)(2,1)S(1)} %collective-permute-done.2.w_z), channel_id=1, source_target_pairs={{0,2},{2,0},{1,3},{3,1},{4,6},{6,4},{5,7},{7,5},{8,10},{10,8},{9,1... | collective-permute-start | bytes 2752520 | tf_op jit(solution)/shard_map/ppermute | solution.py:386
  54.0 12.8 %collective-permute-start.4 = (f32[16,128]{1,0:T(8,128)S(1)}, f32[16,128]{1,0:T(8,128)S(1)}, u32[]{:S(2)}, u32[]{:S(2)}) collective-permute-start(f32[16,128]{1,0:T(8,128)S(1)} %slice.29), channel_id=1, source_target_pairs={{0,8},{2,10},{4,12},{6,14},{8,16},{10,18},{12,20},{14,22},{16,24},... | collective-permute-start | bytes 24584 | tf_op jit(solution)/shard_map/ppermute | solution.py:393

commit v4 on v3

--- a/solution.py
+++ b/solution.py
@@ -63,19 +63,18 @@
     q, first, core, chan, total = info[0], info[1], info[2], info[3], info[4]
     mine = pl.ds(pl.multiple_of(chan * HALF, HALF), HALF)
     theirs = pl.ds(pl.multiple_of((1 - chan) * HALF, HALF), HALF)
-    near = pl.ds(core * 13, 14)
-    far = pl.ds((1 - core) * 13, 14)
-    first_copies = [
-        pltpu.make_async_copy(w_z, w.at[near, :, theirs], sem.at[3]),
-        pltpu.make_async_copy(w_s, w.at[far, :, theirs], sem.at[4]),
-    ]
+    near = pl.ds(pl.multiple_of(core * HALF, HALF), HALF)
+    far = pl.ds(pl.multiple_of((1 - core) * HALF, HALF), HALF)
     copies = []
     for k in range(3):
         taps = pl.ds(9 * k, 9)
-        copies.append(pltpu.make_async_copy(w_own.at[taps], w.at[taps, :, mine], sem.at[k]))
-    first_copies.append(copies[0])
-    for c in first_copies + copies[1:]:
-        c.start()
+        copies.append([
+            pltpu.make_async_copy(w_own.at[taps], w.at[taps, :, mine], sem.at[k, 0]),
+            pltpu.make_async_copy(w_z.at[taps], w.at[taps, near, theirs], sem.at[k, 1]),
+            pltpu.make_async_copy(w_s.at[taps], w.at[taps, far, theirs], sem.at[k, 2]),
+        ])
+        for c in copies[k]:
+            c.start()
 
     def valid(row):
         i = first + row
@@ -120,7 +119,7 @@
     rwin[...] = rcan[pl.ds(start, 112)]
     cot_t = jnp.transpose(ccan[pl.ds(pl.multiple_of(start + 8, OWN), 128)])
 
-    for c in first_copies:
+    for c in copies[0]:
         c.wait()
     ul, va, vb = [None] * 3, [None] * 3, [None] * 3
     for b in range(3):
@@ -158,7 +157,8 @@
             ds0[t - 12] = slope2(p, sil).astype(BF)
         put(pp1, t, ((pair + sil) * valid(row)).astype(BF), 2, 1)
 
-    copies[1].wait()
+    for c in copies[1]:
+        c.wait()
     done = 0
     for t0, n in spans(30, 3):
         while done < t0 + n + 4:
@@ -174,7 +174,8 @@
             pair = pp1[t + 2, :, C : 2 * C].astype(F32)
             put(pp2, t, ((pair + sil) * valid(t - 11)).astype(BF), 4, 1)
 
-    copies[2].wait()
+    for c in copies[2]:
+        c.wait()
 
     half = 0.5 * readout
 
@@ -284,7 +285,7 @@
         vm((128, C), F32),
         vm((64, C), F32),
         vm((64, HALF), F32),
-        pltpu.SemaphoreType.DMA((5,)),
+        pltpu.SemaphoreType.DMA((3, 3)),
     ]
     return pl.pallas_call(
         body,
@@ -318,12 +319,14 @@
     return pairs
 
 
-def copy_taps(core, w_own, out, sem):
+def copy_half(core, w_own, out, sem):
     moves = [
         pltpu.make_async_copy(
-            w_own.at[pl.ds(core[0] * 13 + 2 * k, 2)], out.at[pl.ds(2 * k, 2)], sem.at[k]
+            w_own.at[pl.ds(3 * k, 3), pl.ds(pl.multiple_of(core[0] * HALF, HALF), HALF)],
+            out.at[pl.ds(3 * k, 3)],
+            sem.at[k],
         )
-        for k in range(7)
+        for k in range(9)
     ]
     for move in moves:
         move.start()
@@ -331,15 +334,15 @@
         move.wait()
 
 
-def own_taps(core, w_own):
+def own_part(core, w_own):
     return pl.pallas_call(
-        copy_taps,
-        out_shape=jax.ShapeDtypeStruct((14, C, HALF), BF),
+        copy_half,
+        out_shape=pltpu.VMEM((27, HALF, HALF), BF),
         in_specs=[pl.BlockSpec(memory_space=pltpu.SMEM), pl.BlockSpec(memory_space=pl.ANY)],
         out_specs=pl.BlockSpec(memory_space=pltpu.VMEM),
-        scratch_shapes=[pltpu.SemaphoreType.DMA((7,))],
+        scratch_shapes=[pltpu.SemaphoreType.DMA((9,))],
         cost_estimate=pl.CostEstimate(flops=0, bytes_accessed=2 * 10**6, transcendentals=0),
-        name="own_taps",
+        name="own_part",
     )(core, w_own)
 
 
@@ -359,7 +362,7 @@
     core = lax.axis_index("core")
     chan = lax.axis_index("chan")
     own_w = weight.reshape(27, C, HALF)
-    piece = own_taps(core[None].astype(jnp.int32), own_w)
+    piece = own_part(core[None].astype(jnp.int32), own_w)
     piece, readout, cotangent = lax.optimization_barrier((piece, readout, cotangent))
 
     hi, lo = parts_of(cotangent, 2)

time: 67.8 us -> 66.9 us (0.987)
  Pallas kernels: 13.3 us -> 12.2 us
  waiting for transfers between devices: 11.2 us -> 12.2 us
  starting transfers between devices: 20.3 us -> 19.4 us
    pallas_call x1, Pallas kernels: 2.36 us -> 1.45 us  [own_part(): pl.pallas_call(copy_half, out_shape=pltpu.VMEM((27, HALF, HALF), BF), in_...]
    ppermute x1, waiting for transfers between devices: 7.71 us -> 8.62 us  [local(): moved = lax.ppermute(got[16:32], CHROM, [(b, a) for a, b in next_group])]
    ppermute x1, starting transfers between devices: 4.38 us -> 3.47 us  [local(): moved = lax.ppermute(got[16:32], CHROM, [(b, a) for a, b in next_group])]
where the time goes in v4:
time: 66.9 us; the launch traced here: 66.5 us
  blocking collectives  20.2 us (30%)
  starting transfers between devices  19.4 us (29%)
  Pallas kernels  12.2 us (18%)
  waiting for transfers between devices  12.2 us (18%)
  other arithmetic  1.42 us (2%)
  between operations  0.85 us (1%)
    all_to_all x1, blocking collectives, local(): lax.all_to_all(jnp.broadcast_to(block[None], (8,) + block.shape), GROUP,...  12.7 us
    pallas_call x1, Pallas kernels, local_part(): pl.pallas_call(body, out_shape=jax.ShapeDtypeStruct((8, 64, HALF), BF), i...  10.8 us
    ppermute x1, waiting for transfers between devices, local(): moved = lax.ppermute(got[16:32], CHROM, [(b, a) for a, b in next_group])  8.62 us
    all_to_all x1, blocking collectives, local(): lax.all_to_all(sent, GROUP, 0, 0, tiled=False).astype(F32)  7.45 us
    ppermute x1, starting transfers between devices, local(): after = lax.ppermute(mine, CHROM, next_group)  7.44 us
    ppermute x1, starting transfers between devices, local(): moved = lax.ppermute(got[16:32], CHROM, [(b, a) for a, b in next_group])  3.47 us
    ppermute x1, starting transfers between devices, local(): w_z = lax.ppermute(piece, 'chan', [(0, 1), (1, 0)])  3.37 us
    ppermute x1, starting transfers between devices, local(): edge = lax.ppermute(mine, CHROM, ends)  2.8 us
  transfers between devices with their start and end apart: 5, of which 3 were waited for; matrix products, arithmetic and copies ran while one was open for 1% of the time, Pallas kernels for 0%

profile of v4, /device:TPU:256, one launch (start us, length us, event | category | flops | bytes accessed | tf_op | source)
XLA Modules:
  0.0 66.5 jit_solution(3577309191316740922)
XLA Ops:
  0.6 0.0 copy-start.1
  0.6 0.0 copy-start.4
  0.7 0.0 copy-start.2
  0.7 0.0 copy-start.3
  0.7 0.0 copy-start
  0.7 1.4 %own_part.1 = bf16[27,128,128]{2,1,0:T(8,128)(2,1)S(1)} custom-call(s32[1]{0:T(128)} %bitcast.2.core, bf16[27,256,128]{2,1,0:T(8,128)(2,1)} %bitcast.11), custom_call_target="tpu_custom_call" | custom-call | bytes 2000000 | tf_op jit(solution)/shard_map/own_part/pallas_call | solution.py:338
  2.1 0.0 copy-done.4
  2.2 0.1 reshape.14
  2.3 0.0 copy-done.1
  2.3 0.0 copy-done.2
  2.3 0.0 copy-done.3
  2.3 0.1 fusion.4
  2.4 3.4 %collective-permute-start.2 = (bf16[27,128,128]{2,1,0:T(8,128)(2,1)S(1)}, bf16[27,128,128]{2,1,0:T(8,128)(2,1)}, u32[]{:S(2)}, u32[]{:S(2)}) collective-permute-start(bf16[27,128,128]{2,1,0:T(8,128)(2,1)S(1)} %own_part.1), channel_id=1, source_target_pairs={{0,1},{1,0},{2,3},{3,2},{4,5},{5,4},{6,7},{7,6},{8,9},{9,8},{10,11... | collective-permute-start | bytes 2654216 | tf_op jit(solution)/shard_map/ppermute | solution.py:373
  5.8 7.4 %collective-permute-start = (bf16[48,128]{1,0:T(8,128)(2,1)S(1)}, bf16[48,128]{1,0:T(8,128)(2,1)S(1)}, u32[]{:S(2)}, u32[]{:S(2)}) collective-permute-start(bf16[48,128]{1,0:T(8,128)(2,1)S(1)} %fusion.4), channel_id=1, source_target_pairs={{8,0},{10,2},{12,4},{14,6},{16,8},{18,10},{20,12},{22,14},{24,16},... | collective-permute-start | bytes 36872 | tf_op jit(solution)/shard_map/ppermute | solution.py:381
  13.2 2.8 %collective-permute-start.1 = (bf16[48,128]{1,0:T(8,128)(2,1)S(1)}, bf16[48,128]{1,0:T(8,128)(2,1)S(1)}, u32[]{:S(2)}, u32[]{:S(2)}) collective-permute-start(bf16[48,128]{1,0:T(8,128)(2,1)S(1)} %fusion.4), channel_id=1, source_target_pairs={{6,10},{14,18},{22,26},{30,34},{38,42},{46,50},{54,58},{62,66},{70... | collective-permute-start | bytes 36872 | tf_op jit(solution)/shard_map/ppermute | solution.py:382
  16.0 0.0 collective-permute-done
  16.1 1.3 %collective-permute-done.1 = bf16[48,128]{1,0:T(8,128)(2,1)S(1)} collective-permute-done((bf16[48,128]{1,0:T(8,128)(2,1)S(1)}, bf16[48,128]{1,0:T(8,128)(2,1)S(1)}, u32[]{:S(2)}, u32[]{:S(2)}) %collective-permute-start.1) | collective-permute-done | bytes 12320 | tf_op jit(solution)/shard_map/ppermute | solution.py:382
  17.4 12.7 %all_to_all.10.msg = bf16[8,112,128]{2,1,0:T(8,128)(2,1)S(1)} all-to-all(bf16[8,112,128]{2,1,0:T(8,128)(2,1)S(1)} %broadcast_in_dim.2), channel_id=1, replica_groups=mesh['h'=16,'yh'=4,'yl'=2,'core'=2,'chan'=2] {'yl','core','chan'}, dimensions={0} | all-to-all | bytes 458752 | tf_op jit(solution)/shard_map/all_to_all | solution.py:385
  30.2 0.0 collective-permute-done.2.w_z
  30.2 2.3 %collective-permute-start.3 = (bf16[27,128,128]{2,1,0:T(8,128)(2,1)}, bf16[27,128,128]{2,1,0:T(8,128)(2,1)}, u32[]{:S(2)}, u32[]{:S(2)}) collective-permute-start(bf16[27,128,128]{2,1,0:T(8,128)(2,1)} %collective-permute-done.2.w_z), channel_id=1, source_target_pairs={{0,2},{2,0},{1,3},{3,1},{4,6},{6,4},{5,7},{7,5},{8,10},{10,8},{9,1... | collective-permute-start | bytes 2654216 | tf_op jit(solution)/shard_map/ppermute | solution.py:389
  32.5 0.1 stack.31.info
  32.6 2.3 %collective-permute-done.3.w_s = bf16[27,128,128]{2,1,0:T(8,128)(2,1)} collective-permute-done((bf16[27,128,128]{2,1,0:T(8,128)(2,1)}, bf16[27,128,128]{2,1,0:T(8,128)(2,1)}, u32[]{:S(2)}, u32[]{:S(2)}) %collective-permute-start.3) | collective-permute-done | bytes 884768 | tf_op jit(solution)/shard_map/ppermute | solution.py:389
  34.9 0.0 copy-done
  34.9 10.8 %decoder.1 = bf16[8,64,128]{2,1,0:T(8,128)(2,1)S(1)} custom-call(s32[5]{0:T(128)S(1)} %stack.31.info, bf16[8,112,128]{2,1,0:T(8,128)(2,1)S(1)} %all_to_all.10.msg, bf16[27,256,128]{2,1,0:T(8,128)(2,1)S(1)} %bitcast.12, bf16[27,128,128]{2,1,0:T(8,128)(2,1)} %collective-permute-done.2.w_z, bf16[27,128,128]{2,1,0:T(8,128)(2,1)} %collective-permute-done.3.w_s), custom_call_target="tpu_custom_call" | custom-call | flops 6000000000 | bytes 5000000 | tf_op jit(solution)/shard_map/decoder/pallas_call | solution.py:290
  45.7 7.4 %all_to_all.11 = bf16[8,64,128]{2,1,0:T(8,128)(2,1)S(1)} all-to-all(bf16[8,64,128]{2,1,0:T(8,128)(2,1)S(1)} %decoder.1), channel_id=1, replica_groups=mesh['h'=16,'yh'=4,'yl'=2,'core'=2,'chan'=2] {'yl','core','chan'}, dimensions={0} | all-to-all | bytes 262144 | tf_op jit(solution)/shard_map/all_to_all | solution.py:395
  53.1 3.5 %collective-permute-start.4 = (f32[16,128]{1,0:T(8,128)S(1)}, f32[16,128]{1,0:T(8,128)S(1)}, u32[]{:S(2)}, u32[]{:S(2)}) collective-permute-start(f32[16,128]{1,0:T(8,128)S(1)} %slice.29), channel_id=1, source_target_pairs={{0,8},{2,10},{4,12},{6,14},{8,16},{10,18},{12,20},{14,22},{16,24},... | collective-permute-start | bytes 24584 | tf_op jit(solution)/shard_map/ppermute | solution.py:396
  56.6 0.7 %slice_add_fusion.1 = f32[16,64]{1,0:T(8,128)} fusion(f32[64,128]{1,0:T(8,128)S(1)} %convert_reduce_fusion), kind=kLoop, calls=%fused_computation.15 | loop fusion | flops 1024 | bytes 12288 | tf_op jit(solution)/shard_map/add | solution.py:397
  57.3 8.6 %collective-permute-done.4 = f32[16,128]{1,0:T(8,128)S(1)} collective-permute-done((f32[16,128]{1,0:T(8,128)S(1)}, f32[16,128]{1,0:T(8,128)S(1)}, u32[]{:S(2)}, u32[]{:S(2)}) %collective-permute-start.4) | collective-permute-done | bytes 8224 | tf_op jit(solution)/shard_map/ppermute | solution.py:396
  65.9 0.6 slice_add_fusion
  (9 shorter events, 0.1 us)
Async XLA Ops:
  0.6 1.6 %copy-start.1 = (f32[16,64]{1,0:T(8,128)S(1)}, f32[16,64]{1,0:T(8,128)}, u32[]{:S(2)}) copy-start(f32[16,64]{1,0:T(8,128)} %param.9) | copy-start | bytes 12292
  0.6 1.5 %copy-start.4 = (f32[128]{0:T(128)S(1)}, f32[128]{0:T(128)}, u32[]{:S(2)}) copy-start(f32[128]{0:T(128)} %param.8) | copy-start | bytes 1540
  0.7 1.6 %copy-start.2 = (bf16[16,128]{1,0:T(8,128)(2,1)S(1)}, bf16[16,128]{1,0:T(8,128)(2,1)}, u32[]{:S(2)}) copy-start(bf16[16,128]{1,0:T(8,128)(2,1)} %param.6) | copy-start | bytes 12292
  0.7 1.6 %copy-start.3 = (bf16[16,128]{1,0:T(8,128)(2,1)S(1)}, bf16[16,128]{1,0:T(8,128)(2,1)}, u32[]{:S(2)}) copy-start(bf16[16,128]{1,0:T(8,128)(2,1)} %param.5) | copy-start | bytes 12292
  0.7 34.2 %copy-start = (bf16[3,3,3,256,128]{4,3,2,1,0:T(8,128)(2,1)S(1)}, bf16[3,3,3,256,128]{4,3,2,1,0:T(8,128)(2,1)}, u32[]{:S(2)}) copy-start(bf16[3,3,3,256,128]{4,3,2,1,0:T(8,128)(2,1)} %param.7) | copy-start | bytes 5308420
  2.4 27.8 %collective-permute-start.2 = (bf16[27,128,128]{2,1,0:T(8,128)(2,1)S(1)}, bf16[27,128,128]{2,1,0:T(8,128)(2,1)}, u32[]{:S(2)}, u32[]{:S(2)}) collective-permute-start(bf16[27,128,128]{2,1,0:T(8,128)(2,1)S(1)} %own_part.1), channel_id=1, source_target_pairs={{0,1},{1,0},{2,3},{3,2},{4,5},{5,4},{6,7},{7,6},{8,9},{9,8},{10,11... | collective-permute-start | bytes 2654216 | tf_op jit(solution)/shard_map/ppermute | solution.py:373
  5.8 10.3 %collective-permute-start = (bf16[48,128]{1,0:T(8,128)(2,1)S(1)}, bf16[48,128]{1,0:T(8,128)(2,1)S(1)}, u32[]{:S(2)}, u32[]{:S(2)}) collective-permute-start(bf16[48,128]{1,0:T(8,128)(2,1)S(1)} %fusion.4), channel_id=1, source_target_pairs={{8,0},{10,2},{12,4},{14,6},{16,8},{18,10},{20,12},{22,14},{24,16},... | collective-permute-start | bytes 36872 | tf_op jit(solution)/shard_map/ppermute | solution.py:381
  13.2 4.2 %collective-permute-start.1 = (bf16[48,128]{1,0:T(8,128)(2,1)S(1)}, bf16[48,128]{1,0:T(8,128)(2,1)S(1)}, u32[]{:S(2)}, u32[]{:S(2)}) collective-permute-start(bf16[48,128]{1,0:T(8,128)(2,1)S(1)} %fusion.4), channel_id=1, source_target_pairs={{6,10},{14,18},{22,26},{30,34},{38,42},{46,50},{54,58},{62,66},{70... | collective-permute-start | bytes 36872 | tf_op jit(solution)/shard_map/ppermute | solution.py:382
  30.2 4.7 %collective-permute-start.3 = (bf16[27,128,128]{2,1,0:T(8,128)(2,1)}, bf16[27,128,128]{2,1,0:T(8,128)(2,1)}, u32[]{:S(2)}, u32[]{:S(2)}) collective-permute-start(bf16[27,128,128]{2,1,0:T(8,128)(2,1)} %collective-permute-done.2.w_z), channel_id=1, source_target_pairs={{0,2},{2,0},{1,3},{3,1},{4,6},{6,4},{5,7},{7,5},{8,10},{10,8},{9,1... | collective-permute-start | bytes 2654216 | tf_op jit(solution)/shard_map/ppermute | solution.py:389
  53.1 12.8 %collective-permute-start.4 = (f32[16,128]{1,0:T(8,128)S(1)}, f32[16,128]{1,0:T(8,128)S(1)}, u32[]{:S(2)}, u32[]{:S(2)}) collective-permute-start(f32[16,128]{1,0:T(8,128)S(1)} %slice.29), channel_id=1, source_target_pairs={{0,8},{2,10},{4,12},{6,14},{8,16},{10,18},{12,20},{14,22},{16,24},... | collective-permute-start | bytes 24584 | tf_op jit(solution)/shard_map/ppermute | solution.py:396

commit v5 on v4

--- a/solution.py
+++ b/solution.py
@@ -131,12 +131,12 @@
                 va[b] = y[40:]
             else:
                 vb[b] = y[40:] if a == 1 else vb[b] + y[40:]
-    u_all[...] = ul[0] + ul[1] + ul[2]
+    u_all[...] = 0.5 * (ul[0] + ul[1] + ul[2])
     for var in range(2):
         v = [vb[b] + va[b] if var == 0 else vb[b] for b in range(3)]
-        v_all[var] = v[0] + v[1] + v[2]
-        e0[var] = ul[1] + ul[2] + (v[1] + v[2])[:40]
-        e63[var] = ul[0] + ul[1] + (v[0] + v[1])[63:103]
+        v_all[var] = 0.5 * (v[0] + v[1] + v[2])
+        e0[var] = 0.5 * (ul[1] + ul[2] + (v[1] + v[2])[:40])
+        e63[var] = 0.5 * (ul[0] + ul[1] + (v[0] + v[1])[63:103])
     tile = lax.broadcasted_iota(jnp.int32, (8, C), 0)
 
     def row_0(t):
@@ -152,10 +152,10 @@
             ],
             axis=0,
         )
-        p, sil = gate(0.5 * pre)
+        p, sil = gate(pre)
         if 12 <= t < 22:
             ds0[t - 12] = slope2(p, sil).astype(BF)
-        put(pp1, t, ((pair + sil) * valid(row)).astype(BF), 2, 1)
+        put(pp1, t, (pair + sil).astype(BF) * valid(row).astype(BF), 2, 1)
 
     for c in copies[1]:
         c.wait()
@@ -172,7 +172,7 @@
             if 8 <= t < 22:
                 ds1[t - 8] = slope2(p, sil).astype(BF)
             pair = pp1[t + 2, :, C : 2 * C].astype(F32)
-            put(pp2, t, ((pair + sil) * valid(t - 11)).astype(BF), 4, 1)
+            put(pp2, t, (pair + sil).astype(BF) * valid(t - 11).astype(BF), 4, 1)
 
     for c in copies[2]:
         c.wait()

time: 66.9 us -> 66.7 us (level)
  no operation moved by 1% of the time
where the time goes in v5:
time: 66.7 us; the launch traced here: 66.3 us
  blocking collectives  20.2 us (30%)
  starting transfers between devices  19.4 us (29%)
  waiting for transfers between devices  12.2 us (18%)
  Pallas kernels  12.1 us (18%)
  other arithmetic  1.42 us (2%)
  between operations  0.85 us (1%)
    all_to_all x1, blocking collectives, local(): lax.all_to_all(jnp.broadcast_to(block[None], (8,) + block.shape), GROUP,...  12.7 us
    pallas_call x1, Pallas kernels, local_part(): pl.pallas_call(body, out_shape=jax.ShapeDtypeStruct((8, 64, HALF), BF), i...  10.6 us
    ppermute x1, waiting for transfers between devices, local(): moved = lax.ppermute(got[16:32], CHROM, [(b, a) for a, b in next_group])  8.63 us
    all_to_all x1, blocking collectives, local(): lax.all_to_all(sent, GROUP, 0, 0, tiled=False).astype(F32)  7.45 us
    ppermute x1, starting transfers between devices, local(): after = lax.ppermute(mine, CHROM, next_group)  7.44 us
    ppermute x1, starting transfers between devices, local(): moved = lax.ppermute(got[16:32], CHROM, [(b, a) for a, b in next_group])  3.46 us
    ppermute x1, starting transfers between devices, local(): w_z = lax.ppermute(piece, 'chan', [(0, 1), (1, 0)])  3.37 us
    ppermute x1, starting transfers between devices, local(): edge = lax.ppermute(mine, CHROM, ends)  2.8 us
  transfers between devices with their start and end apart: 5, of which 3 were waited for; matrix products, arithmetic and copies ran while one was open for 1% of the time, Pallas kernels for 0%

profile of v5, /device:TPU:256, one launch (start us, length us, event | category | flops | bytes accessed | tf_op | source)
XLA Modules:
  0.0 66.3 jit_solution(8472555307536179334)
XLA Ops:
  0.6 0.0 copy-start.1
  0.6 0.0 copy-start.4
  0.7 0.0 copy-start.2
  0.7 0.0 copy-start.3
  0.7 0.0 copy-start
  0.7 1.4 %own_part.1 = bf16[27,128,128]{2,1,0:T(8,128)(2,1)S(1)} custom-call(s32[1]{0:T(128)} %bitcast.2.core, bf16[27,256,128]{2,1,0:T(8,128)(2,1)} %bitcast.11), custom_call_target="tpu_custom_call" | custom-call | bytes 2000000 | tf_op jit(solution)/shard_map/own_part/pallas_call | solution.py:338
  2.1 0.0 copy-done.4
  2.2 0.1 reshape.14
  2.3 0.0 copy-done.1
  2.3 0.0 copy-done.2
  2.3 0.0 copy-done.3
  2.3 0.1 fusion.4
  2.4 3.4 %collective-permute-start.2 = (bf16[27,128,128]{2,1,0:T(8,128)(2,1)S(1)}, bf16[27,128,128]{2,1,0:T(8,128)(2,1)}, u32[]{:S(2)}, u32[]{:S(2)}) collective-permute-start(bf16[27,128,128]{2,1,0:T(8,128)(2,1)S(1)} %own_part.1), channel_id=1, source_target_pairs={{0,1},{1,0},{2,3},{3,2},{4,5},{5,4},{6,7},{7,6},{8,9},{9,8},{10,11... | collective-permute-start | bytes 2654216 | tf_op jit(solution)/shard_map/ppermute | solution.py:373
  5.8 7.4 %collective-permute-start = (bf16[48,128]{1,0:T(8,128)(2,1)S(1)}, bf16[48,128]{1,0:T(8,128)(2,1)S(1)}, u32[]{:S(2)}, u32[]{:S(2)}) collective-permute-start(bf16[48,128]{1,0:T(8,128)(2,1)S(1)} %fusion.4), channel_id=1, source_target_pairs={{8,0},{10,2},{12,4},{14,6},{16,8},{18,10},{20,12},{22,14},{24,16},... | collective-permute-start | bytes 36872 | tf_op jit(solution)/shard_map/ppermute | solution.py:381
  13.2 2.8 %collective-permute-start.1 = (bf16[48,128]{1,0:T(8,128)(2,1)S(1)}, bf16[48,128]{1,0:T(8,128)(2,1)S(1)}, u32[]{:S(2)}, u32[]{:S(2)}) collective-permute-start(bf16[48,128]{1,0:T(8,128)(2,1)S(1)} %fusion.4), channel_id=1, source_target_pairs={{6,10},{14,18},{22,26},{30,34},{38,42},{46,50},{54,58},{62,66},{70... | collective-permute-start | bytes 36872 | tf_op jit(solution)/shard_map/ppermute | solution.py:382
  16.0 0.0 collective-permute-done
  16.1 1.3 %collective-permute-done.1 = bf16[48,128]{1,0:T(8,128)(2,1)S(1)} collective-permute-done((bf16[48,128]{1,0:T(8,128)(2,1)S(1)}, bf16[48,128]{1,0:T(8,128)(2,1)S(1)}, u32[]{:S(2)}, u32[]{:S(2)}) %collective-permute-start.1) | collective-permute-done | bytes 12320 | tf_op jit(solution)/shard_map/ppermute | solution.py:382
  17.4 12.7 %all_to_all.10.msg = bf16[8,112,128]{2,1,0:T(8,128)(2,1)S(1)} all-to-all(bf16[8,112,128]{2,1,0:T(8,128)(2,1)S(1)} %broadcast_in_dim.2), channel_id=1, replica_groups=mesh['h'=16,'yh'=4,'yl'=2,'core'=2,'chan'=2] {'yl','core','chan'}, dimensions={0} | all-to-all | bytes 458752 | tf_op jit(solution)/shard_map/all_to_all | solution.py:385
  30.2 0.0 collective-permute-done.2.w_z
  30.2 2.3 %collective-permute-start.3 = (bf16[27,128,128]{2,1,0:T(8,128)(2,1)}, bf16[27,128,128]{2,1,0:T(8,128)(2,1)}, u32[]{:S(2)}, u32[]{:S(2)}) collective-permute-start(bf16[27,128,128]{2,1,0:T(8,128)(2,1)} %collective-permute-done.2.w_z), channel_id=1, source_target_pairs={{0,2},{2,0},{1,3},{3,1},{4,6},{6,4},{5,7},{7,5},{8,10},{10,8},{9,1... | collective-permute-start | bytes 2654216 | tf_op jit(solution)/shard_map/ppermute | solution.py:389
  32.5 0.1 stack.31.info
  32.6 2.3 %collective-permute-done.3.w_s = bf16[27,128,128]{2,1,0:T(8,128)(2,1)} collective-permute-done((bf16[27,128,128]{2,1,0:T(8,128)(2,1)}, bf16[27,128,128]{2,1,0:T(8,128)(2,1)}, u32[]{:S(2)}, u32[]{:S(2)}) %collective-permute-start.3) | collective-permute-done | bytes 884768 | tf_op jit(solution)/shard_map/ppermute | solution.py:389
  34.9 0.0 copy-done
  34.9 10.6 %decoder.1 = bf16[8,64,128]{2,1,0:T(8,128)(2,1)S(1)} custom-call(s32[5]{0:T(128)S(1)} %stack.31.info, bf16[8,112,128]{2,1,0:T(8,128)(2,1)S(1)} %all_to_all.10.msg, bf16[27,256,128]{2,1,0:T(8,128)(2,1)S(1)} %bitcast.12, bf16[27,128,128]{2,1,0:T(8,128)(2,1)} %collective-permute-done.2.w_z, bf16[27,128,128]{2,1,0:T(8,128)(2,1)} %collective-permute-done.3.w_s), custom_call_target="tpu_custom_call" | custom-call | flops 6000000000 | bytes 5000000 | tf_op jit(solution)/shard_map/decoder/pallas_call | solution.py:290
  45.5 7.4 %all_to_all.11 = bf16[8,64,128]{2,1,0:T(8,128)(2,1)S(1)} all-to-all(bf16[8,64,128]{2,1,0:T(8,128)(2,1)S(1)} %decoder.1), channel_id=1, replica_groups=mesh['h'=16,'yh'=4,'yl'=2,'core'=2,'chan'=2] {'yl','core','chan'}, dimensions={0} | all-to-all | bytes 262144 | tf_op jit(solution)/shard_map/all_to_all | solution.py:395
  53.0 3.5 %collective-permute-start.4 = (f32[16,128]{1,0:T(8,128)S(1)}, f32[16,128]{1,0:T(8,128)S(1)}, u32[]{:S(2)}, u32[]{:S(2)}) collective-permute-start(f32[16,128]{1,0:T(8,128)S(1)} %slice.29), channel_id=1, source_target_pairs={{0,8},{2,10},{4,12},{6,14},{8,16},{10,18},{12,20},{14,22},{16,24},... | collective-permute-start | bytes 24584 | tf_op jit(solution)/shard_map/ppermute | solution.py:396
  56.4 0.7 %slice_add_fusion.1 = f32[16,64]{1,0:T(8,128)} fusion(f32[64,128]{1,0:T(8,128)S(1)} %convert_reduce_fusion), kind=kLoop, calls=%fused_computation.15 | loop fusion | flops 1024 | bytes 12288 | tf_op jit(solution)/shard_map/add | solution.py:397
  57.1 8.6 %collective-permute-done.4 = f32[16,128]{1,0:T(8,128)S(1)} collective-permute-done((f32[16,128]{1,0:T(8,128)S(1)}, f32[16,128]{1,0:T(8,128)S(1)}, u32[]{:S(2)}, u32[]{:S(2)}) %collective-permute-start.4) | collective-permute-done | bytes 8224 | tf_op jit(solution)/shard_map/ppermute | solution.py:396
  65.7 0.6 slice_add_fusion
  (9 shorter events, 0.1 us)
Async XLA Ops:
  0.6 1.6 %copy-start.1 = (f32[16,64]{1,0:T(8,128)S(1)}, f32[16,64]{1,0:T(8,128)}, u32[]{:S(2)}) copy-start(f32[16,64]{1,0:T(8,128)} %param.9) | copy-start | bytes 12292
  0.6 1.5 %copy-start.4 = (f32[128]{0:T(128)S(1)}, f32[128]{0:T(128)}, u32[]{:S(2)}) copy-start(f32[128]{0:T(128)} %param.8) | copy-start | bytes 1540
  0.7 1.6 %copy-start.2 = (bf16[16,128]{1,0:T(8,128)(2,1)S(1)}, bf16[16,128]{1,0:T(8,128)(2,1)}, u32[]{:S(2)}) copy-start(bf16[16,128]{1,0:T(8,128)(2,1)} %param.6) | copy-start | bytes 12292
  0.7 1.6 %copy-start.3 = (bf16[16,128]{1,0:T(8,128)(2,1)S(1)}, bf16[16,128]{1,0:T(8,128)(2,1)}, u32[]{:S(2)}) copy-start(bf16[16,128]{1,0:T(8,128)(2,1)} %param.5) | copy-start | bytes 12292
  0.7 34.2 %copy-start = (bf16[3,3,3,256,128]{4,3,2,1,0:T(8,128)(2,1)S(1)}, bf16[3,3,3,256,128]{4,3,2,1,0:T(8,128)(2,1)}, u32[]{:S(2)}) copy-start(bf16[3,3,3,256,128]{4,3,2,1,0:T(8,128)(2,1)} %param.7) | copy-start | bytes 5308420
  2.4 27.8 %collective-permute-start.2 = (bf16[27,128,128]{2,1,0:T(8,128)(2,1)S(1)}, bf16[27,128,128]{2,1,0:T(8,128)(2,1)}, u32[]{:S(2)}, u32[]{:S(2)}) collective-permute-start(bf16[27,128,128]{2,1,0:T(8,128)(2,1)S(1)} %own_part.1), channel_id=1, source_target_pairs={{0,1},{1,0},{2,3},{3,2},{4,5},{5,4},{6,7},{7,6},{8,9},{9,8},{10,11... | collective-permute-start | bytes 2654216 | tf_op jit(solution)/shard_map/ppermute | solution.py:373
  5.8 10.3 %collective-permute-start = (bf16[48,128]{1,0:T(8,128)(2,1)S(1)}, bf16[48,128]{1,0:T(8,128)(2,1)S(1)}, u32[]{:S(2)}, u32[]{:S(2)}) collective-permute-start(bf16[48,128]{1,0:T(8,128)(2,1)S(1)} %fusion.4), channel_id=1, source_target_pairs={{8,0},{10,2},{12,4},{14,6},{16,8},{18,10},{20,12},{22,14},{24,16},... | collective-permute-start | bytes 36872 | tf_op jit(solution)/shard_map/ppermute | solution.py:381
  13.2 4.2 %collective-permute-start.1 = (bf16[48,128]{1,0:T(8,128)(2,1)S(1)}, bf16[48,128]{1,0:T(8,128)(2,1)S(1)}, u32[]{:S(2)}, u32[]{:S(2)}) collective-permute-start(bf16[48,128]{1,0:T(8,128)(2,1)S(1)} %fusion.4), channel_id=1, source_target_pairs={{6,10},{14,18},{22,26},{30,34},{38,42},{46,50},{54,58},{62,66},{70... | collective-permute-start | bytes 36872 | tf_op jit(solution)/shard_map/ppermute | solution.py:382
  30.2 4.7 %collective-permute-start.3 = (bf16[27,128,128]{2,1,0:T(8,128)(2,1)}, bf16[27,128,128]{2,1,0:T(8,128)(2,1)}, u32[]{:S(2)}, u32[]{:S(2)}) collective-permute-start(bf16[27,128,128]{2,1,0:T(8,128)(2,1)} %collective-permute-done.2.w_z), channel_id=1, source_target_pairs={{0,2},{2,0},{1,3},{3,1},{4,6},{6,4},{5,7},{7,5},{8,10},{10,8},{9,1... | collective-permute-start | bytes 2654216 | tf_op jit(solution)/shard_map/ppermute | solution.py:389
  53.0 12.8 %collective-permute-start.4 = (f32[16,128]{1,0:T(8,128)S(1)}, f32[16,128]{1,0:T(8,128)S(1)}, u32[]{:S(2)}, u32[]{:S(2)}) collective-permute-start(f32[16,128]{1,0:T(8,128)S(1)} %slice.29), channel_id=1, source_target_pairs={{0,8},{2,10},{4,12},{6,14},{8,16},{10,18},{12,20},{14,22},{16,24},... | collective-permute-start | bytes 24584 | tf_op jit(solution)/shard_map/ppermute | solution.py:396

commit v6 on v5

--- a/solution.py
+++ b/solution.py
@@ -8,7 +8,7 @@
 BF = jnp.bfloat16
 F32 = jnp.float32
 CHROM = ("h", "yh", "yl", "core")
-GROUP = ("yl", "core", "chan")
+GROUP = ("chan", "yl", "core")
 ALL = CHROM + ("chan",)
 BAND = 64
 C = 256
@@ -88,7 +88,7 @@
 
     for j in range(4):
         for g in range(2):
-            e = 2 * j + g
+            e = 4 * g + j
             lanes = slice(HALF * g, HALF * g + HALF)
             place(lcan, 16 + 16 * j, lanes, msg[e, 0:16])
             place(rcan, 16 + 16 * j, lanes, msg[e, 16:32])
@@ -101,11 +101,11 @@
             if j == 3:
                 place(rcan, 144, lanes, msg[e, 80:96])
     for to, j, at in ((0, 1, 96), (16, 0, 32), (32, 1, 32), (48, 2, 32), (64, 3, 32), (80, 0, 96)):
-        ccan[to : to + 16] = msg[2 * j, at : at + 16].astype(F32) + msg[2 * j + 1, at : at + 16].astype(F32)
+        ccan[to : to + 16] = msg[j, at : at + 16].astype(F32) + msg[4 + j, at : at + 16].astype(F32)
     halves = []
     lane = lax.broadcasted_iota(jnp.int32, (1, HALF), 1)
     for g in range(2):
-        m = msg[g, 32:48].astype(F32)
+        m = msg[4 * g, 32:48].astype(F32)
         even, odd = m[0:1] + m[2:3] + m[4:5], m[1:2] + m[3:4] + m[5:6]
         halves.append(jnp.where(lane < BAND, pltpu.roll(even, BAND, 1), odd))
     readout = jnp.concatenate(halves, axis=1)
@@ -252,10 +252,10 @@
     for j in range(4):
         for g in range(2):
             lanes = slice(HALF * g, HALF * g + HALF)
-            out[2 * j + g, 0:16] = rcv[16 * j : 16 * j + 16, lanes].astype(BF)
-            out[2 * j + g, 16:32] = rcv[64 + 16 * j : 80 + 16 * j, lanes].astype(BF)
-            out[2 * j + g, 32:48] = lcv[16 * j : 16 * j + 16, lanes].astype(BF)
-            out[2 * j + g, 48:64] = ccv[16 * j : 16 * j + 16].astype(BF)
+            out[4 * g + j, 0:16] = rcv[16 * j : 16 * j + 16, lanes].astype(BF)
+            out[4 * g + j, 16:32] = rcv[64 + 16 * j : 80 + 16 * j, lanes].astype(BF)
+            out[4 * g + j, 32:48] = lcv[16 * j : 16 * j + 16, lanes].astype(BF)
+            out[4 * g + j, 48:64] = ccv[16 * j : 16 * j + 16].astype(BF)
 
 
 def local_part(info, msg, w_own, w_z, w_s):
@@ -387,7 +387,7 @@
     )
     msg, w_z = lax.optimization_barrier((msg, w_z))
     w_s = lax.ppermute(w_z, "core", [(0, 1), (1, 0)])
-    q = lax.axis_index(GROUP)
+    q = lax.axis_index(("yl", "core", "chan"))
     info = jnp.stack(
         [q, rows * slab + OWN * chan, core, chan, rows * chroms]
     ).astype(jnp.int32)

time: 66.7 us -> 68 us (1.019)
  blocking collectives: 20.2 us -> 21.5 us
  waiting for transfers between devices: 12.2 us -> 13.4 us
  starting transfers between devices: 19.4 us -> 18.2 us
    all_to_all x1, blocking collectives: 12.7 us -> 13.6 us  [local(): lax.all_to_all(jnp.broadcast_to(block[None], (8,) + block.shape), GROUP,...]
    ppermute x1, waiting for transfers between devices: 8.63 us -> 9.38 us  [local(): moved = lax.ppermute(got[16:32], CHROM, [(b, a) for a, b in next_group])]
    ppermute x1, starting transfers between devices: 3.46 us -> 2.71 us  [local(): moved = lax.ppermute(got[16:32], CHROM, [(b, a) for a, b in next_group])]
where the time goes in v6:
time: 68 us; the launch traced here: 67.7 us
  blocking collectives  21.5 us (32%)
  starting transfers between devices  18.2 us (27%)
  waiting for transfers between devices  13.4 us (20%)
  Pallas kernels  12 us (18%)
  other arithmetic  1.42 us (2%)
  between operations  0.85 us (1%)
    all_to_all x1, blocking collectives, local(): lax.all_to_all(jnp.broadcast_to(block[None], (8,) + block.shape), GROUP,...  13.6 us
    pallas_call x1, Pallas kernels, local_part(): pl.pallas_call(body, out_shape=jax.ShapeDtypeStruct((8, 64, HALF), BF), i...  10.6 us
    ppermute x1, waiting for transfers between devices, local(): moved = lax.ppermute(got[16:32], CHROM, [(b, a) for a, b in next_group])  9.38 us
    all_to_all x1, blocking collectives, local(): lax.all_to_all(sent, GROUP, 0, 0, tiled=False).astype(F32)  7.92 us
    ppermute x1, starting transfers between devices, local(): after = lax.ppermute(mine, CHROM, next_group)  7.44 us
    ppermute x1, starting transfers between devices, local(): w_z = lax.ppermute(piece, 'chan', [(0, 1), (1, 0)])  3.37 us
    ppermute x1, starting transfers between devices, local(): edge = lax.ppermute(mine, CHROM, ends)  2.8 us
    ppermute x1, starting transfers between devices, local(): moved = lax.ppermute(got[16:32], CHROM, [(b, a) for a, b in next_group])  2.71 us
  transfers between devices with their start and end apart: 5, of which 3 were waited for; matrix products, arithmetic and copies ran while one was open for 1% of the time, Pallas kernels for 0%

profile of v6, /device:TPU:256, one launch (start us, length us, event | category | flops | bytes accessed | tf_op | source)
XLA Modules:
  0.0 67.7 jit_solution(6858278373014130291)
XLA Ops:
  0.6 0.0 copy-start.1
  0.6 0.0 copy-start.4
  0.7 0.0 copy-start.2
  0.7 0.0 copy-start.3
  0.7 0.0 copy-start
  0.7 1.4 %own_part.1 = bf16[27,128,128]{2,1,0:T(8,128)(2,1)S(1)} custom-call(s32[1]{0:T(128)} %bitcast.2.core, bf16[27,256,128]{2,1,0:T(8,128)(2,1)} %bitcast.11), custom_call_target="tpu_custom_call" | custom-call | bytes 2000000 | tf_op jit(solution)/shard_map/own_part/pallas_call | solution.py:338
  2.1 0.0 copy-done.4
  2.2 0.1 reshape.14
  2.3 0.0 copy-done.1
  2.3 0.0 copy-done.2
  2.3 0.0 copy-done.3
  2.3 0.1 fusion.4
  2.4 3.4 %collective-permute-start.2 = (bf16[27,128,128]{2,1,0:T(8,128)(2,1)S(1)}, bf16[27,128,128]{2,1,0:T(8,128)(2,1)}, u32[]{:S(2)}, u32[]{:S(2)}) collective-permute-start(bf16[27,128,128]{2,1,0:T(8,128)(2,1)S(1)} %own_part.1), channel_id=1, source_target_pairs={{0,1},{1,0},{2,3},{3,2},{4,5},{5,4},{6,7},{7,6},{8,9},{9,8},{10,11... | collective-permute-start | bytes 2654216 | tf_op jit(solution)/shard_map/ppermute | solution.py:373
  5.8 7.4 %collective-permute-start = (bf16[48,128]{1,0:T(8,128)(2,1)S(1)}, bf16[48,128]{1,0:T(8,128)(2,1)S(1)}, u32[]{:S(2)}, u32[]{:S(2)}) collective-permute-start(bf16[48,128]{1,0:T(8,128)(2,1)S(1)} %fusion.4), channel_id=1, source_target_pairs={{8,0},{10,2},{12,4},{14,6},{16,8},{18,10},{20,12},{22,14},{24,16},... | collective-permute-start | bytes 36872 | tf_op jit(solution)/shard_map/ppermute | solution.py:381
  13.2 2.8 %collective-permute-start.1 = (bf16[48,128]{1,0:T(8,128)(2,1)S(1)}, bf16[48,128]{1,0:T(8,128)(2,1)S(1)}, u32[]{:S(2)}, u32[]{:S(2)}) collective-permute-start(bf16[48,128]{1,0:T(8,128)(2,1)S(1)} %fusion.4), channel_id=1, source_target_pairs={{6,10},{14,18},{22,26},{30,34},{38,42},{46,50},{54,58},{62,66},{70... | collective-permute-start | bytes 36872 | tf_op jit(solution)/shard_map/ppermute | solution.py:382
  16.0 0.0 collective-permute-done
  16.1 1.3 %collective-permute-done.1 = bf16[48,128]{1,0:T(8,128)(2,1)S(1)} collective-permute-done((bf16[48,128]{1,0:T(8,128)(2,1)S(1)}, bf16[48,128]{1,0:T(8,128)(2,1)S(1)}, u32[]{:S(2)}, u32[]{:S(2)}) %collective-permute-start.1) | collective-permute-done | bytes 12320 | tf_op jit(solution)/shard_map/ppermute | solution.py:382
  17.4 13.6 %all_to_all.10.msg = bf16[8,112,128]{2,1,0:T(8,128)(2,1)S(1)} all-to-all(bf16[8,112,128]{2,1,0:T(8,128)(2,1)S(1)} %broadcast_in_dim.2), channel_id=1, replica_groups=mesh['h'=16,'yh'=4,'yl'=2,'core'=2,'chan'=2] {'chan','yl','core'}, dimensions={0} | all-to-all | bytes 458752 | tf_op jit(solution)/shard_map/all_to_all | solution.py:385
  31.1 0.0 collective-permute-done.2.w_z
  31.1 1.9 %collective-permute-start.3 = (bf16[27,128,128]{2,1,0:T(8,128)(2,1)}, bf16[27,128,128]{2,1,0:T(8,128)(2,1)}, u32[]{:S(2)}, u32[]{:S(2)}) collective-permute-start(bf16[27,128,128]{2,1,0:T(8,128)(2,1)} %collective-permute-done.2.w_z), channel_id=1, source_target_pairs={{0,2},{2,0},{1,3},{3,1},{4,6},{6,4},{5,7},{7,5},{8,10},{10,8},{9,1... | collective-permute-start | bytes 2654216 | tf_op jit(solution)/shard_map/ppermute | solution.py:389
  33.0 0.1 stack.31.info
  33.1 2.6 %collective-permute-done.3.w_s = bf16[27,128,128]{2,1,0:T(8,128)(2,1)} collective-permute-done((bf16[27,128,128]{2,1,0:T(8,128)(2,1)}, bf16[27,128,128]{2,1,0:T(8,128)(2,1)}, u32[]{:S(2)}, u32[]{:S(2)}) %collective-permute-start.3) | collective-permute-done | bytes 884768 | tf_op jit(solution)/shard_map/ppermute | solution.py:389
  35.7 0.0 copy-done
  35.7 10.6 %decoder.1 = bf16[8,64,128]{2,1,0:T(8,128)(2,1)S(1)} custom-call(s32[5]{0:T(128)S(1)} %stack.31.info, bf16[8,112,128]{2,1,0:T(8,128)(2,1)S(1)} %all_to_all.10.msg, bf16[27,256,128]{2,1,0:T(8,128)(2,1)S(1)} %bitcast.12, bf16[27,128,128]{2,1,0:T(8,128)(2,1)} %collective-permute-done.2.w_z, bf16[27,128,128]{2,1,0:T(8,128)(2,1)} %collective-permute-done.3.w_s), custom_call_target="tpu_custom_call" | custom-call | flops 6000000000 | bytes 5000000 | tf_op jit(solution)/shard_map/decoder/pallas_call | solution.py:290
  46.3 7.9 %all_to_all.11 = bf16[8,64,128]{2,1,0:T(8,128)(2,1)S(1)} all-to-all(bf16[8,64,128]{2,1,0:T(8,128)(2,1)S(1)} %decoder.1), channel_id=1, replica_groups=mesh['h'=16,'yh'=4,'yl'=2,'core'=2,'chan'=2] {'chan','yl','core'}, dimensions={0} | all-to-all | bytes 262144 | tf_op jit(solution)/shard_map/all_to_all | solution.py:395
  54.3 2.7 %collective-permute-start.4 = (f32[16,128]{1,0:T(8,128)S(1)}, f32[16,128]{1,0:T(8,128)S(1)}, u32[]{:S(2)}, u32[]{:S(2)}) collective-permute-start(f32[16,128]{1,0:T(8,128)S(1)} %slice.29), channel_id=1, source_target_pairs={{0,8},{2,10},{4,12},{6,14},{8,16},{10,18},{12,20},{14,22},{16,24},... | collective-permute-start | bytes 24584 | tf_op jit(solution)/shard_map/ppermute | solution.py:396
  57.0 0.7 slice_add_fusion.1
  57.7 9.4 %collective-permute-done.4 = f32[16,128]{1,0:T(8,128)S(1)} collective-permute-done((f32[16,128]{1,0:T(8,128)S(1)}, f32[16,128]{1,0:T(8,128)S(1)}, u32[]{:S(2)}, u32[]{:S(2)}) %collective-permute-start.4) | collective-permute-done | bytes 8224 | tf_op jit(solution)/shard_map/ppermute | solution.py:396
  67.1 0.6 slice_add_fusion
  (9 shorter events, 0.1 us)
Async XLA Ops:
  0.6 1.6 %copy-start.1 = (f32[16,64]{1,0:T(8,128)S(1)}, f32[16,64]{1,0:T(8,128)}, u32[]{:S(2)}) copy-start(f32[16,64]{1,0:T(8,128)} %param.9) | copy-start | bytes 12292
  0.6 1.5 %copy-start.4 = (f32[128]{0:T(128)S(1)}, f32[128]{0:T(128)}, u32[]{:S(2)}) copy-start(f32[128]{0:T(128)} %param.8) | copy-start | bytes 1540
  0.7 1.6 %copy-start.2 = (bf16[16,128]{1,0:T(8,128)(2,1)S(1)}, bf16[16,128]{1,0:T(8,128)(2,1)}, u32[]{:S(2)}) copy-start(bf16[16,128]{1,0:T(8,128)(2,1)} %param.6) | copy-start | bytes 12292
  0.7 1.6 %copy-start.3 = (bf16[16,128]{1,0:T(8,128)(2,1)S(1)}, bf16[16,128]{1,0:T(8,128)(2,1)}, u32[]{:S(2)}) copy-start(bf16[16,128]{1,0:T(8,128)(2,1)} %param.5) | copy-start | bytes 12292
  0.7 35.0 %copy-start = (bf16[3,3,3,256,128]{4,3,2,1,0:T(8,128)(2,1)S(1)}, bf16[3,3,3,256,128]{4,3,2,1,0:T(8,128)(2,1)}, u32[]{:S(2)}) copy-start(bf16[3,3,3,256,128]{4,3,2,1,0:T(8,128)(2,1)} %param.7) | copy-start | bytes 5308420
  2.4 28.7 %collective-permute-start.2 = (bf16[27,128,128]{2,1,0:T(8,128)(2,1)S(1)}, bf16[27,128,128]{2,1,0:T(8,128)(2,1)}, u32[]{:S(2)}, u32[]{:S(2)}) collective-permute-start(bf16[27,128,128]{2,1,0:T(8,128)(2,1)S(1)} %own_part.1), channel_id=1, source_target_pairs={{0,1},{1,0},{2,3},{3,2},{4,5},{5,4},{6,7},{7,6},{8,9},{9,8},{10,11... | collective-permute-start | bytes 2654216 | tf_op jit(solution)/shard_map/ppermute | solution.py:373
  5.8 10.3 %collective-permute-start = (bf16[48,128]{1,0:T(8,128)(2,1)S(1)}, bf16[48,128]{1,0:T(8,128)(2,1)S(1)}, u32[]{:S(2)}, u32[]{:S(2)}) collective-permute-start(bf16[48,128]{1,0:T(8,128)(2,1)S(1)} %fusion.4), channel_id=1, source_target_pairs={{8,0},{10,2},{12,4},{14,6},{16,8},{18,10},{20,12},{22,14},{24,16},... | collective-permute-start | bytes 36872 | tf_op jit(solution)/shard_map/ppermute | solution.py:381
  13.2 4.2 %collective-permute-start.1 = (bf16[48,128]{1,0:T(8,128)(2,1)S(1)}, bf16[48,128]{1,0:T(8,128)(2,1)S(1)}, u32[]{:S(2)}, u32[]{:S(2)}) collective-permute-start(bf16[48,128]{1,0:T(8,128)(2,1)S(1)} %fusion.4), channel_id=1, source_target_pairs={{6,10},{14,18},{22,26},{30,34},{38,42},{46,50},{54,58},{62,66},{70... | collective-permute-start | bytes 36872 | tf_op jit(solution)/shard_map/ppermute | solution.py:382
  31.1 4.7 %collective-permute-start.3 = (bf16[27,128,128]{2,1,0:T(8,128)(2,1)}, bf16[27,128,128]{2,1,0:T(8,128)(2,1)}, u32[]{:S(2)}, u32[]{:S(2)}) collective-permute-start(bf16[27,128,128]{2,1,0:T(8,128)(2,1)} %collective-permute-done.2.w_z), channel_id=1, source_target_pairs={{0,2},{2,0},{1,3},{3,1},{4,6},{6,4},{5,7},{7,5},{8,10},{10,8},{9,1... | collective-permute-start | bytes 2654216 | tf_op jit(solution)/shard_map/ppermute | solution.py:389
  54.3 12.8 %collective-permute-start.4 = (f32[16,128]{1,0:T(8,128)S(1)}, f32[16,128]{1,0:T(8,128)S(1)}, u32[]{:S(2)}, u32[]{:S(2)}) collective-permute-start(f32[16,128]{1,0:T(8,128)S(1)} %slice.29), channel_id=1, source_target_pairs={{0,8},{2,10},{4,12},{6,14},{8,16},{10,18},{12,20},{14,22},{16,24},... | collective-permute-start | bytes 24584 | tf_op jit(solution)/shard_map/ppermute | solution.py:396
